TPU v7x, 256 devices: a whole 4x4x8 slice. The times are simulated.
256 devices in a mesh: island: 16 (over y_hi, x, core), fsdp: 16 (over y_lo, z).
Axes of the slice: x: 4, y: 4 (y_hi: 2, y_lo: 2; y = y_hi * 2 + y_lo), z: 8, core: 2. Of those that a mesh axis runs over, the one named last changes fastest.
Arguments:
- normed: bfloat16 [2, 49152, 8192], P(None, ('island', 'fsdp')), may hold values from -6 to 6
- value_weight: bfloat16 [16, 8192, 512], P('island', 'fsdp'), may hold values from -0.0625 to 0.0625
- value_cotangent: bfloat16 [2, 49152, 512], P(None, ('island', 'fsdp')), may hold values from -0.079589844 to 0.079589844
- local_fragment: bfloat16 [16, 8192, 512], P('island', 'fsdp'), may hold values from -6 to 6
- global_fragment: float32 [8192, 512], P('fsdp'), may hold values from -6 to 6
- outer_momentum: float32 [8192, 512], P('fsdp', 'island'), may hold values from -3 to 3
Outputs:
- projected: bfloat16 [2, 49152, 512], P(None, ('island', 'fsdp'))
- value_grad: float32 [16, 8192, 512], P('island', 'fsdp')
- new_global: float32 [8192, 512], P('fsdp')
- new_momentum: float32 [8192, 512], P('fsdp', 'island')
All inputs are finite; a program needn't handle non-finite values.
Results may differ from a plain program's by a relative error of at most 0.001.
Values may be sent and summed in bfloat16 or wider, within the bound.
No kernel may reach another device: no remote copies, remote signals or barrier semaphores. Data moves between devices by JAX's collectives and lax.ppermute only.
A program may use at most 128 MiB of HBM per device.

v0:
```python
import jax
import jax.numpy as jnp
from jax import lax
from jax.sharding import PartitionSpec as P

outer_rate = 0.7
outer_mu = 0.9


def per_device(
    normed, value_weight, value_cotangent, local_fragment, global_fragment, outer_momentum
):
    micro_count, tok_rows, model_width = normed.shape
    kv_width = value_cotangent.shape[2]
    flat_rows = normed.reshape(micro_count * tok_rows, model_width)
    flat_cots = value_cotangent.reshape(micro_count * tok_rows, kv_width)
    columns = flat_rows
    forward = jnp.dot(
        columns,
        lax.all_gather(value_weight[0], "fsdp", axis=0, tiled=True),
        preferred_element_type=jnp.float32,
    )
    projected = forward.astype(jnp.bfloat16).reshape(micro_count, tok_rows, kv_width)
    columns = flat_rows
    gradient = lax.psum_scatter(
        lax.dot_general(
            columns, flat_cots, (((0,), (0,)), ((), ())), preferred_element_type=jnp.float32
        ),
        "fsdp",
        scatter_dimension=0,
        tiled=True,
    )
    value_grad = gradient[None]
    islands = lax.axis_size("island")
    own_delta = global_fragment - local_fragment[0].astype(jnp.float32)
    col_width = outer_momentum.shape[1]
    position = lax.axis_index("island")
    pseudo = lax.psum(own_delta, "island") / islands
    shared = lax.dynamic_slice_in_dim(pseudo, position * col_width, col_width, 1)
    new_momentum = outer_mu * outer_momentum + shared
    full_momentum = lax.all_gather(new_momentum, "island", axis=1, tiled=True)
    new_global = global_fragment - outer_rate * (pseudo + outer_mu * full_momentum)
    return (projected, value_grad, new_global, new_momentum)


def solution(mesh):
    placed = (
        P(None, ("island", "fsdp"), None),
        P("island", "fsdp", None),
        P(None, ("island", "fsdp"), None),
        P("island", "fsdp", None),
        P("fsdp", None),
        P("fsdp", "island"),
    )
    return jax.shard_map(
        per_device,
        mesh=mesh,
        in_specs=placed,
        out_specs=(
            P(None, ("island", "fsdp"), None),
            P("island", "fsdp", None),
            P("fsdp", None),
            P("fsdp", "island"),
        ),
        check_vma=False,
    )
```

profile of v0, /device:TPU:1, one launch (start us, length us, event | category | flops | bytes accessed | tf_op | source)
XLA Modules:
  0.0 510.5 jit_solution(15630123859144068690)
XLA Ops:
  7.2 0.0 copy-start
  7.2 0.0 copy-start.2
  7.2 0.0 all-reduce.2.cloned.1.call-start
  7.2 1.6 copy.12
  8.8 1.3 copy.10
  10.1 1.1 convert_subtract_fusion
  11.2 0.0 all-reduce.2.cloned.1.call-update
  11.3 0.0 all-gather.4.cloned.1.call-start
  11.3 149.2 %all-reduce.2.cloned.1.call-done = f32[512,512]{0,1:T(8,128)} async-done(((f32[512,512]{0,1:T(8,128)}), f32[512,512]{0,1:T(8,128)}) %all-reduce.2.cloned.1.call-update) | async-done | bytes 1048592 | tf_op jit(solution)/shard_map/psum | solution.py:38
  160.5 1.3 broadcast_multiply_fusion
  161.8 0.0 copy-done.2
  161.8 0.6 dynamic-slice_add_fusion
  162.5 0.0 all-gather.4.cloned.1.call-update
  162.5 0.0 all-gather.6.cloned.1.call-start
  162.6 0.7 all-gather.6.cloned.1.call-update
  163.2 0.0 reduce-scatter.2.cloned.1.call-start
  163.3 0.0 copy-done
  163.3 11.1 %convolution_bitcast_fusion = f32[8192,512]{1,0:T(8,128)} fusion(bf16[2,192,8192]{2,1,0:T(8,128)(2,1)} %param.6, bf16[2,192,512]{2,1,0:T(8,128)(2,1)S(1)} %copy-done), kind=kOutput, calls=%fused_computation | convolution fusion | flops 3221225472 | bytes 23461888 | tf_op jit(solution)/shard_map/dot_general | solution.py:26
  174.4 0.0 copy-start.1
  174.4 0.0 reduce-scatter.2.cloned.1.call-update
  174.4 41.6 %all-gather.4.cloned.1.call-done = f32[512,512]{0,1:T(8,128)} async-done(((f32[512,32]{0,1:T(8,128)}), f32[512,512]{0,1:T(8,128)}) %all-gather.4.cloned.1.call-update) | async-done | bytes 1048592 | tf_op jit(solution)/shard_map/all_gather | solution.py:41
  216.0 0.0 copy-done.1
  216.0 1.6 multiply_subtract_fusion
  217.6 1.3 copy.13
  218.9 98.5 %all-gather.6.cloned.1.call-done = bf16[1,8192,512]{2,1,0:T(8,128)(2,1)} async-done(((bf16[1,512,512]{2,1,0:T(8,128)(2,1)}), bf16[1,8192,512]{2,1,0:T(8,128)(2,1)}) %all-gather.6.cloned.1.call-update) | async-done | bytes 8388624 | tf_op jit(solution)/shard_map/all_gather | solution.py:20
  317.4 9.3 %fusion.2 = bf16[384,512]{1,0:T(8,128)(2,1)} fusion(bf16[384,8192]{1,0:T(8,128)(2,1)} %bitcast.16, bf16[1,8192,512]{2,1,0:T(8,128)(2,1)} %all-gather.6.cloned.1.call-done), kind=kOutput, calls=%fused_computation.3 | convolution fusion | flops 3221422080 | bytes 15073280 | tf_op jit(solution)/shard_map/dot_general | solution.py:18
  326.7 177.3 %reduce-scatter.2.cloned.1.call-done = f32[512,512]{1,0:T(8,128)} async-done(((f32[8192,512]{1,0:T(8,128)}), f32[512,512]{1,0:T(8,128)}) %reduce-scatter.2.cloned.1.call-update) | async-done | bytes 1048592 | tf_op jit(solution)/shard_map/reduce_scatter | solution.py:25
Async XLA Ops:
  7.2 156.1 %copy-start = (bf16[2,192,512]{2,1,0:T(8,128)(2,1)S(1)}, bf16[2,192,512]{2,1,0:T(8,128)(2,1)}, u32[]{:S(2)}) copy-start(bf16[2,192,512]{2,1,0:T(8,128)(2,1)} %param.8) | copy-start | bytes 1179652
  7.2 154.7 %copy-start.2 = (f32[512,32]{0,1:T(8,128)S(1)}, f32[512,32]{0,1:T(8,128)}, u32[]{:S(2)}) copy-start(f32[512,32]{0,1:T(8,128)} %param.11) | copy-start | bytes 196612
  7.2 153.3 %all-reduce.2.cloned.1.call-start = ((), (), s32[]{:S(2)}) async-start(), calls=%async_computation.2 | async-start | bytes 2097152 | tf_op jit(solution)/shard_map/psum | solution.py:38
  11.3 204.7 %all-gather.4.cloned.1.call-start = ((), (), s32[]{:S(2)}) async-start(), calls=%async_computation.3 | async-start | bytes 1114112 | tf_op jit(solution)/shard_map/all_gather | solution.py:41
  162.5 154.9 %all-gather.6.cloned.1.call-start = ((), (), s32[]{:S(2)}) async-start(), calls=%async_computation.4 | async-start | bytes 8912896 | tf_op jit(solution)/shard_map/all_gather | solution.py:20
  163.2 340.7 %reduce-scatter.2.cloned.1.call-start = ((), (), s32[]{:S(2)}) async-start(), calls=%async_computation.1 | async-start | bytes 17825792 | tf_op jit(solution)/shard_map/reduce_scatter | solution.py:25
  174.4 41.6 %copy-start.1 = (f32[512,512]{0,1:T(8,128)S(1)}, f32[512,512]{0,1:T(8,128)}, u32[]{:S(2)}) copy-start(f32[512,512]{0,1:T(8,128)} %all-reduce.2.cloned.1.call-done) | copy-start | bytes 3145732
Sparse Core Ops, SparseCore 0:
  11.4 149.0 all-reduce.1
  164.2 51.7 all-gather.3
  217.9 99.4 all-gather.5
  320.5 183.4 reduce-scatter.1
where the time goes:
time: 511 us
  waiting for transfers between devices  467 us (91%)
  matrix products  20.4 us (4%)
  between operations  13.8 us (3%)
    reduce_scatter x1, waiting for transfers between devices, per_device(): lax.psum_scatter(lax.dot_general(columns, flat_cots, (((0,), (0,)), ((),...  177 us
    psum x1, waiting for transfers between devices, per_device(): pseudo = lax.psum(own_delta, 'island') / islands  149 us
    all_gather x1, waiting for transfers between devices, per_device(): lax.all_gather(value_weight[0], 'fsdp', axis=0, tiled=True)  98.5 us
    all_gather x1, waiting for transfers between devices, per_device(): full_momentum = lax.all_gather(new_momentum, 'island', axis=1, tiled=True)  41.6 us
    dot_general x1, matrix products, per_device(): lax.dot_general(columns, flat_cots, (((0,), (0,)), ((), ())), preferred_e...  11.1 us
  transfers between devices with their start and end apart: 4, of which 4 were waited for; matrix products, arithmetic and copies ran while one was open for 5% of the time, Pallas kernels for 0%

commit v1 on v0

v1 whole, which is shorter than its diff:
```python
import jax
import jax.numpy as jnp
from jax import lax
from jax.sharding import PartitionSpec as P

outer_rate = 0.7
outer_mu = 0.9

Z = 8
PAIR = [(i, (i + Z) % (2 * Z)) for i in range(2 * Z)]
UP = [(i, i // Z * Z + (i + 1) % Z) for i in range(2 * Z)]
DOWN = [(i, i // Z * Z + (i - 1) % Z) for i in range(2 * Z)]
ROWS = [list(range(Z)), list(range(Z, 2 * Z))]
ORDER = (4, -3, 3, -2, 2, -1, 1, 0)
f32 = jnp.float32


def xor(bit):
    return [(i, i ^ bit) for i in range(16)]


def after(x, *deps):
    return lax.optimization_barrier((x, *deps))[0]


def pick(a, i, axis):
    return lax.dynamic_index_in_dim(a, i, axis, keepdims=False)


def outer_step(local, global_fragment, outer_momentum):
    island = lax.axis_index("island").astype(jnp.uint32)
    bits = [(island >> b) & 1 for b in range(4)]
    cols = outer_momentum.shape[1]
    rows = local.shape[0]
    part = local.T.reshape(2, 2, 2, 2, cols, rows)
    for b in range(4):
        sent = pick(part, 1 - bits[b], 3 - b)
        part = pick(part, bits[b], 3 - b).astype(f32) + lax.ppermute(sent, "island", xor(1 << b)).astype(f32)
    mine = lax.dynamic_slice_in_dim(global_fragment, island * cols, cols, 1).T
    pseudo = mine - part / 16
    momentum = outer_mu * outer_momentum.T + pseudo
    full = mine - outer_rate * (pseudo + outer_mu * momentum)
    for b in (3, 2, 1, 0):
        got = lax.ppermute(full, "island", xor(1 << b))
        low = bits[b] == 0
        full = jnp.stack([jnp.where(low, full, got), jnp.where(low, got, full)], 3 - b)
    return full.reshape(-1, rows).T, momentum.T


def per_device(
    normed, value_weight, value_cotangent, local_fragment, global_fragment, outer_momentum
):
    micro_count, tok_rows, model_width = normed.shape
    kv = value_cotangent.shape[2]
    tokens = micro_count * tok_rows
    half = model_width // 2
    chunk = half // Z
    n = normed.reshape(tokens, model_width)
    c = value_cotangent.reshape(tokens, kv)
    fsdp = lax.axis_index("fsdp").astype(jnp.uint32)
    yl, z = fsdp >> 3, fsdp & 7
    spots = [((z + (o & 7)) & 7) * chunk for o in ORDER]

    w_half = lax.all_gather(value_weight[0], "fsdp", axis=0, tiled=True, axis_index_groups=ROWS)

    c_p = lax.ppermute(c, "fsdp", PAIR)
    got = []
    for s in range(Z):
        cut = lax.dynamic_slice_in_dim(n, (1 - yl) * half + spots[s], chunk, 1)
        if s >= 2:
            cut = after(cut, got[s - 2])
        elif s == 1:
            cut = after(cut, c_p)
        got.append(lax.ppermute(cut, "fsdp", PAIR))

    bound = jnp.max(jnp.abs(n)).astype(f32) * jnp.max(jnp.abs(c)).astype(f32)
    bound = jnp.full((8, 128), bound)
    for perm in (PAIR, xor(1), xor(2), xor(4)):
        bound = jnp.maximum(bound, lax.ppermute(bound, "fsdp", perm))
    bound = jnp.maximum(bound[0, 0] * (tokens * 2 * Z), 1e-33)
    scale, unscale = 32768.0 / bound, bound / 32768.0

    def tn(a, b):
        return lax.dot_general(a, b, (((0,), (0,)), ((), ())), preferred_element_type=f32)

    n_half = lax.dynamic_slice_in_dim(n, yl * half, half, 1)
    own = tn(n_half, c)
    up = down = None
    for s in range(Z):
        g = lax.dynamic_slice_in_dim(own, spots[s], chunk, 0) + tn(got[s], c_p)
        g = g * scale
        o = ORDER[s]
        if o > 0:
            if up is not None:
                g = g + up.astype(f32)
            up = lax.ppermute(g.astype(jnp.float16), "fsdp", UP)
        elif o < 0:
            if down is not None:
                g = g + down.astype(f32)
            down = lax.ppermute(g.astype(jnp.float16), "fsdp", DOWN)
        else:
            g = g + up.astype(f32) + down.astype(f32)
    value_grad = (g * unscale)[None]

    theirs = jnp.zeros((tokens, kv), f32)
    for s in range(Z):
        ws = lax.dynamic_slice_in_dim(w_half, spots[s], chunk, 0)
        theirs = theirs + jnp.dot(got[s], ws, preferred_element_type=f32)
    mine = jnp.dot(n_half, w_half, preferred_element_type=f32)
    projected = mine + lax.ppermute(theirs, "fsdp", PAIR)
    projected = projected.astype(jnp.bfloat16).reshape(micro_count, tok_rows, kv)

    new_global, new_momentum = outer_step(local_fragment[0], global_fragment, outer_momentum)
    return (projected, value_grad, new_global, new_momentum)


def solution(mesh):
    placed = (
        P(None, ("island", "fsdp"), None),
        P("island", "fsdp", None),
        P(None, ("island", "fsdp"), None),
        P("island", "fsdp", None),
        P("fsdp", None),
        P("fsdp", "island"),
    )
    return jax.shard_map(
        per_device,
        mesh=mesh,
        in_specs=placed,
        out_specs=(
            P(None, ("island", "fsdp"), None),
            P("island", "fsdp", None),
            P("fsdp", None),
            P("fsdp", "island"),
        ),
        check_vma=False,
    )
```

time: 511 us -> 146 us (0.29)
  waiting for transfers between devices: 467 us -> 32.9 us
  starting transfers between devices: 0.16 us -> 46.8 us
  matrix products: 20.4 us -> 33.3 us
    reduce_scatter x1 -> x0, waiting for transfers between devices: 177 us -> none  [per_device(): lax.psum_scatter(lax.dot_general(columns, flat_cots, (((0,), (0,)), ((),...]
    psum x1 -> x0, waiting for transfers between devices: 149 us -> none  [per_device(): pseudo = lax.psum(own_delta, 'island') / islands]
    all_gather x2 -> x1, waiting for transfers between devices: 140 us -> 0.02 us  [per_device(): lax.all_gather(value_weight[0], 'fsdp', axis=0, tiled=True, axis_index_gr...]
    ppermute x0 -> x29, starting transfers between devices: none -> 46.8 us  [the longest x4 11.9 us: outer_step(): got = lax.ppermute(full, 'island', xor(1 << b))]
    ppermute x0 -> x29, waiting for transfers between devices: none -> 32.2 us  [the longest x4 12.2 us: outer_step(): got = lax.ppermute(full, 'island', xor(1 << b))]
    dot_general x2 -> x18, matrix products: 20.4 us -> 33.3 us  [the longest x9 19.8 us: tn(): lax.dot_general(a, b, (((0,), (0,)), ((), ())), preferred_element_type=f32)]
  transfers between devices with their start and end apart: 4 -> 30, of which waited for: 4 -> 8; matrix products, arithmetic and copies ran while one was open for 5% -> 32% of each run, Pallas kernels for 0% -> 0%
where the time goes in v1:
time: 146 us; the launch traced here: 145 us
  starting transfers between devices  46.8 us (32%)
  matrix products  33.3 us (23%)
  waiting for transfers between devices  32.9 us (23%)
  between operations  16.5 us (11%)
  other arithmetic  9 us (6%)
  local copies, waits for them, and re-layouts  6.84 us (5%)
    dot_general x9, matrix products, tn(): lax.dot_general(a, b, (((0,), (0,)), ((), ())), preferred_element_type=f32)  19.8 us
    ppermute x4, waiting for transfers between devices, outer_step(): got = lax.ppermute(full, 'island', xor(1 << b))  12.2 us
    ppermute x4, starting transfers between devices, outer_step(): got = lax.ppermute(full, 'island', xor(1 << b))  11.9 us
    ppermute x4, starting transfers between devices, outer_step(): lax.ppermute(sent, 'island', xor(1 << b)).astype(f32)  9.81 us
    ppermute x3, starting transfers between devices, per_device(): down = lax.ppermute(g.astype(jnp.float16), 'fsdp', DOWN)  9.07 us
    dot_general x8, matrix products, per_device(): theirs = theirs + jnp.dot(got[s], ws, preferred_element_type=f32)  8.66 us
    ppermute x4, starting transfers between devices, per_device(): bound = jnp.maximum(bound, lax.ppermute(bound, 'fsdp', perm))  7.36 us
    ppermute x8, starting transfers between devices, per_device(): got.append(lax.ppermute(cut, 'fsdp', PAIR))  5.96 us
  transfers between devices with their start and end apart: 30, of which 8 were waited for; matrix products, arithmetic and copies ran while one was open for 32% of the time, Pallas kernels for 0%

profile of v1, /device:TPU:1, one launch (start us, length us, event | category | flops | bytes accessed | tf_op | source)
XLA Modules:
  0.0 145.4 jit_solution(18013546140946968141)
XLA Ops:
  9.2 3.3 %collective-permute-start.21 = (bf16[2,2,2,32,512]{4,3,2,1,0:T(8,128)(2,1)S(1)}, bf16[2,2,2,32,512]{4,3,2,1,0:T(8,128)(2,1)S(1)}, u32[]{:S(2)}, u32[]{:S(2)}) collective-permute-start(bf16[2,2,2,32,512]{4,3,2,1,0:T(8,128)(2,1)S(1)} %dynamic-slice_bitcast_fusion.1), channel_id=1, source_target_pairs={{0,16},{16,0},{32,48},{48,32},{64,80},{80,64},{96,112},{112,96},{1... | collective-permute-start | bytes 786440 | tf_op jit(solution)/shard_map/ppermute | solution.py:38
  12.6 4.2 %abs_reduce_fusion = bf16[]{:T(256)} fusion(bf16[2,192,8192]{2,1,0:T(8,128)(2,1)} %param.6), kind=kLoop, calls=%fused_computation | loop fusion | flops 6291455 | bytes 6291458 | tf_op jit(solution)/shard_map/reduce_max | solution.py:76
  18.8 1.5 collective-permute-start.1
  22.6 3.4 %constant_dynamic-slice_fusion.8 = (bf16[384,512]{1,0:T(8,128)(2,1)}, bf16[384,512]{1,0:T(8,128)(2,1)}, bf16[384,512]{1,0:T(8,128)(2,1)}, bf16[384,512]{1,0:T(8,...) fusion(bf16[384,8192]{1,0:T(8,128)(2,1)} %bitcast.129, ...), kind=kLoop, calls=%fused_computation.112 | loop fusion | bytes 6291488 | tf_op jit(solution)/shard_map/dynamic_slice | solution.py:69
  27.3 3.0 %collective-permute-start.12 = (f32[8,128]{1,0:T(8,128)S(1)}, f32[8,128]{1,0:T(8,128)S(1)}, u32[]{:S(2)}, u32[]{:S(2)}) collective-permute-start(f32[8,128]{1,0:T(8,128)S(1)} %fusion.96), channel_id=1, source_target_pairs={{0,2},{1,3},{2,0},{3,1},{4,6},{5,7},{6,4},{7,5},{8,10},{9,11},{10,... | collective-permute-start | bytes 12296 | tf_op jit(solution)/shard_map/ppermute | solution.py:79
  31.3 2.5 %collective-permute-start.23 = (f32[2,32,512]{2,1,0:T(8,128)S(1)}, f32[2,32,512]{2,1,0:T(8,128)S(1)}, u32[]{:S(2)}, u32[]{:S(2)}) collective-permute-start(f32[2,32,512]{2,1,0:T(8,128)S(1)} %dynamic-slice_bitcast_fusion.2), channel_id=1, source_target_pairs={{0,64},{16,80},{32,96},{48,112},{64,0},{80,16},{96,32},{112,48},{1... | collective-permute-start | bytes 393224 | tf_op jit(solution)/shard_map/ppermute | solution.py:38
  33.8 7.6 %fusion.2 = f32[4096,512]{1,0:T(8,128)} fusion(bf16[384,512]{1,0:T(8,128)(2,1)S(1)} %bitcast.136, bf16[384,8192]{1,0:T(8,128)(2,1)} %bitcast.130, u32[]{:T(128)S(6)} %mul.102), kind=kOutput, calls=%fused_computation.3 | convolution fusion | flops 1610612736 | bytes 11927556 | tf_op jit(solution)/shard_map/dot_general | solution.py:84
  41.4 4.3 %collective-permute-start.13 = (f32[8,128]{1,0:T(8,128)S(1)}, f32[8,128]{1,0:T(8,128)S(1)}, u32[]{:S(2)}, u32[]{:S(2)}) collective-permute-start(f32[8,128]{1,0:T(8,128)S(1)} %max.18), channel_id=1, source_target_pairs={{0,4},{1,5},{2,6},{3,7},{4,0},{5,1},{6,2},{7,3},{8,12},{9,13},{10,... | collective-permute-start | bytes 12296 | tf_op jit(solution)/shard_map/ppermute | solution.py:79
  45.8 2.8 %collective-permute-start.24 = (f32[32,512]{1,0:T(8,128)S(1)}, f32[32,512]{1,0:T(8,128)S(1)}, u32[]{:S(2)}, u32[]{:S(2)}) collective-permute-start(f32[32,512]{1,0:T(8,128)S(1)} %dynamic-slice_bitcast_fusion.3), channel_id=1, source_target_pairs={{0,128},{16,144},{32,160},{48,176},{64,192},{80,208},{96,224},{112... | collective-permute-start | bytes 196616 | tf_op jit(solution)/shard_map/ppermute | solution.py:38
  52.2 2.0 %collective-permute-start.25 = (f32[32,512]{1,0:T(8,128)S(1)}, f32[32,512]{1,0:T(8,128)S(1)}, u32[]{:S(2)}, u32[]{:S(2)}) collective-permute-start(f32[32,512]{1,0:T(8,128)S(1)} %get-tuple-element.35), channel_id=1, source_target_pairs={{0,128},{16,144},{32,160},{48,176},{64,192},{80,208},{96,224},{112... | collective-permute-start | bytes 196616 | tf_op jit(solution)/shard_map/ppermute | solution.py:44
  54.2 1.7 %fusion.22 = f16[512,512]{1,0:T(8,128)(2,1)S(1)} fusion(bf16[384,512]{1,0:T(8,128)(2,1)S(1)} %collective-permute-done, bf16[384,512]{1,0:T(8,128)(2,1)S(1)} %collective-permute-done.1, f32[4096,512]{1,0:T(8,128)} %fusion.2, u32[]{:T(128)S(6)} %mul.104, f32[]{:T(128)} %bitcast.12), kind=kOutput, calls=%fused_computation.31 | convolution fusion | flops 202113024 | bytes 2359304 | tf_op jit(solution)/shard_map/dot_general | solution.py:84
  56.6 11.4 %collective-permute-done.25 = f32[32,512]{1,0:T(8,128)S(1)} collective-permute-done((f32[32,512]{1,0:T(8,128)S(1)}, f32[32,512]{1,0:T(8,128)S(1)}, u32[]{:S(2)}, u32[]{:S(2)}) %collective-permute-start.25) | collective-permute-done | bytes 65568 | tf_op jit(solution)/shard_map/ppermute | solution.py:44
  70.2 1.9 %fusion.23 = f16[512,512]{1,0:T(8,128)(2,1)S(1)} fusion(bf16[384,512]{1,0:T(8,128)(2,1)S(1)} %collective-permute-done.2, bf16[384,512]{1,0:T(8,128)(2,1)S(1)} %collective-permute-done.1, f32[4096,512]{1,0:T(8,128)} %fusion.2, u32[]{:T(128)S(6)} %mul.105, f32[]{:T(128)} %bitcast.12), kind=kOutput, calls=%fused_computation.32 | convolution fusion | flops 202113024 | bytes 2359304 | tf_op jit(solution)/shard_map/dot_general | solution.py:84
  72.1 2.7 %collective-permute-start.18 = (f16[512,512]{1,0:T(8,128)(2,1)S(1)}, f16[512,512]{1,0:T(8,128)(2,1)S(1)}, u32[]{:S(2)}, u32[]{:S(2)}) collective-permute-start(f16[512,512]{1,0:T(8,128)(2,1)S(1)} %fusion.23), channel_id=1, source_target_pairs={{0,7},{1,0},{2,1},{3,2},{4,3},{5,4},{6,5},{7,6},{8,15},{9,8},{10,9... | collective-permute-start | bytes 1572872 | tf_op jit(solution)/shard_map/ppermute | solution.py:100
  74.9 1.5 %collective-permute-start.27 = (f32[2,2,32,512]{3,2,1,0:T(8,128)S(1)}, f32[2,2,32,512]{3,2,1,0:T(8,128)S(1)}, u32[]{:S(2)}, u32[]{:S(2)}) collective-permute-start(f32[2,2,32,512]{3,2,1,0:T(8,128)S(1)} %pad_maximum_fusion.2), channel_id=1, source_target_pairs={{0,32},{16,48},{32,0},{48,16},{64,96},{80,112},{96,64},{112,80},{1... | collective-permute-start | bytes 786440 | tf_op jit(solution)/shard_map/ppermute | solution.py:44
  76.3 1.5 %collective-permute-done.14 = f16[512,512]{1,0:T(8,128)(2,1)S(1)} collective-permute-done((f16[512,512]{1,0:T(8,128)(2,1)S(1)}, f16[512,512]{1,0:T(8,128)(2,1)S(1)}, u32[]{:S(2)}, u32[]{:S(2)}) %collective-permute-start.14) | collective-permute-done | bytes 524320 | tf_op jit(solution)/shard_map/ppermute | solution.py:96
  77.9 1.7 %fusion.32 = f16[512,512]{1,0:T(8,128)(2,1)S(1)} fusion(bf16[384,512]{1,0:T(8,128)(2,1)S(1)} %collective-permute-done.3, bf16[384,512]{1,0:T(8,128)(2,1)S(1)} %collective-permute-done.1, f16[512,512]{1,0:T(8,128)(2,1)S(1)} %collective-permute-done.14, f32[4096,512]{1,0:T(8,128)} %fusion.2, u32[]{:T(128)S(6)} %mul.106, f32[]{:T(128)} %bitcast.12), kind=kOutput, calls=%fused_computation.42 | convolution fusion | flops 202637312 | bytes 2883592 | tf_op jit(solution)/shard_map/dot_general | solution.py:84
  80.6 7.9 %collective-permute-start.28 = (f32[2,2,2,32,512]{4,3,2,1,0:T(8,128)S(1)}, f32[2,2,2,32,512]{4,3,2,1,0:T(8,128)S(1)}, u32[]{:S(2)}, u32[]{:S(2)}) collective-permute-start(f32[2,2,2,32,512]{4,3,2,1,0:T(8,128)S(1)} %pad_maximum_fusion.1), channel_id=1, source_target_pairs={{0,16},{16,0},{32,48},{48,32},{64,80},{80,64},{96,112},{112,96},{1... | collective-permute-start | bytes 1572872 | tf_op jit(solution)/shard_map/ppermute | solution.py:44
  88.5 1.5 %collective-permute-start.7 = (bf16[384,512]{1,0:T(8,128)(2,1)}, bf16[384,512]{1,0:T(8,128)(2,1)S(1)}, u32[]{:S(2)}, u32[]{:S(2)}) collective-permute-start(bf16[384,512]{1,0:T(8,128)(2,1)} %get-tuple-element.16), channel_id=1, source_target_pairs={{0,8},{1,9},{2,10},{3,11},{4,12},{5,13},{6,14},{7,15},{8,0},{9,1},... | collective-permute-start | bytes 1179656 | tf_op jit(solution)/shard_map/ppermute | solution.py:74
  90.5 2.9 %collective-permute-start.19 = (f16[512,512]{1,0:T(8,128)(2,1)S(1)}, f16[512,512]{1,0:T(8,128)(2,1)S(1)}, u32[]{:S(2)}, u32[]{:S(2)}) collective-permute-start(f16[512,512]{1,0:T(8,128)(2,1)S(1)} %fusion.34), channel_id=1, source_target_pairs={{0,7},{1,0},{2,1},{3,2},{4,3},{5,4},{6,5},{7,6},{8,15},{9,8},{10,9... | collective-permute-start | bytes 1572872 | tf_op jit(solution)/shard_map/ppermute | solution.py:100
  94.1 5.1 %collective-permute-done.6 = bf16[384,512]{1,0:T(8,128)(2,1)S(1)} collective-permute-done((bf16[384,512]{1,0:T(8,128)(2,1)S(1)}, bf16[384,512]{1,0:T(8,128)(2,1)S(1)}, u32[]{:S(2)}, u32[]{:S(2)}) %collective-permute-start.6) | collective-permute-done | bytes 393248 | tf_op jit(solution)/shard_map/ppermute | solution.py:74
  99.4 4.6 %collective-permute-done.19 = f16[512,512]{1,0:T(8,128)(2,1)S(1)} collective-permute-done((f16[512,512]{1,0:T(8,128)(2,1)S(1)}, f16[512,512]{1,0:T(8,128)(2,1)S(1)}, u32[]{:S(2)}, u32[]{:S(2)}) %collective-permute-start.19) | collective-permute-done | bytes 524320 | tf_op jit(solution)/shard_map/ppermute | solution.py:100
  105.4 3.4 %collective-permute-start.20 = (f16[512,512]{1,0:T(8,128)(2,1)}, f16[512,512]{1,0:T(8,128)(2,1)}, u32[]{:S(2)}, u32[]{:S(2)}) collective-permute-start(f16[512,512]{1,0:T(8,128)(2,1)} %fusion.33), channel_id=1, source_target_pairs={{0,7},{1,0},{2,1},{3,2},{4,3},{5,4},{6,5},{7,6},{8,15},{9,8},{10,9... | collective-permute-start | bytes 1572872 | tf_op jit(solution)/shard_map/ppermute | solution.py:100
  110.2 1.7 %fusion.37 = f32[384,512]{1,0:T(8,128)S(1)} fusion(bf16[384,512]{1,0:T(8,128)(2,1)} %copy-done.11, bf16[1,4096,512]{2,1,0:T(8,128)(2,1)} %all-gather.3.cloned.1.call-done, u32[]{:T(128)S(6)} %mul.110), kind=kOutput, calls=%fused_computation.51 | convolution fusion | flops 201326592 | bytes 1703940 | tf_op jit(solution)/shard_map/dot_general | solution.py:108
  111.9 1.6 %fusion.39 = f32[384,512]{1,0:T(8,128)S(1)} fusion(bf16[384,512]{1,0:T(8,128)(2,1)} %copy-done.10, bf16[1,4096,512]{2,1,0:T(8,128)(2,1)} %all-gather.3.cloned.1.call-done, u32[]{:T(128)S(6)} %mul.109), kind=kOutput, calls=%fused_computation.53 | convolution fusion | flops 201326592 | bytes 1703940 | tf_op jit(solution)/shard_map/dot_general | solution.py:108
  113.5 1.5 %fusion.41 = f32[384,512]{1,0:T(8,128)S(1)} fusion(bf16[384,512]{1,0:T(8,128)(2,1)} %copy-done.9, bf16[1,4096,512]{2,1,0:T(8,128)(2,1)} %all-gather.3.cloned.1.call-done, u32[]{:T(128)S(6)} %mul.108), kind=kOutput, calls=%fused_computation.55 | convolution fusion | flops 201326592 | bytes 1703940 | tf_op jit(solution)/shard_map/dot_general | solution.py:108
  117.6 1.4 fusion.29
  120.7 2.6 %collective-permute-done.17 = f16[512,512]{1,0:T(8,128)(2,1)} collective-permute-done((f16[512,512]{1,0:T(8,128)(2,1)}, f16[512,512]{1,0:T(8,128)(2,1)}, u32[]{:S(2)}, u32[]{:S(2)}) %collective-permute-start.17) | collective-permute-done | bytes 524320 | tf_op jit(solution)/shard_map/ppermute | solution.py:96
  123.3 3.2 %fusion.21 = f32[1,512,512]{2,1,0:T(8,128)} fusion(bf16[384,512]{1,0:T(8,128)(2,1)} %copy-done.3, bf16[384,512]{1,0:T(8,128)(2,1)S(1)} %collective-permute-done.1, f16[512,512]{1,0:T(8,128)(2,1)} %collective-permute-done.20, f16[512,512]{1,0:T(8,128)(2,1)} %collective-permute-done.17, f32[4096,512]{1,0:T(8,128)} %fusion.2, u32[]{:T(128)S(6)} %mul.111, ...), kind=kOutput, calls=%fused_computation.30 | convolution fusion | flops 203161600 | bytes 3932172 | tf_op jit(solution)/shard_map/dot_general | solution.py:84
  126.5 4.9 %fusion = f32[384,512]{1,0:T(8,128)S(1)} fusion(bf16[1,4096,512]{2,1,0:T(8,128)(2,1)} %all-gather.3.cloned.1.call-done, bf16[384,8192]{1,0:T(8,128)(2,1)} %bitcast.131, u32[]{:T(128)S(6)} %mul.102), kind=kOutput, calls=%fused_computation.1 | convolution fusion | flops 1610612736 | bytes 8126468 | tf_op jit(solution)/shard_map/dot_general | solution.py:109
  131.4 5.1 %collective-permute-done.9 = f32[384,512]{1,0:T(8,128)} collective-permute-done((f32[384,512]{1,0:T(8,128)}, f32[384,512]{1,0:T(8,128)}, u32[]{:S(2)}, u32[]{:S(2)}) %collective-permute-start.9) | collective-permute-done | bytes 786464 | tf_op jit(solution)/shard_map/ppermute | solution.py:110
  136.5 2.0 %add_convert_fusion = bf16[384,512]{1,0:T(8,128)(2,1)} fusion(f32[384,512]{1,0:T(8,128)S(1)} %fusion, f32[384,512]{1,0:T(8,128)} %collective-permute-done.9), kind=kLoop, calls=%fused_computation.46 | loop fusion | flops 393216 | bytes 1966080 | tf_op jit(solution)/shard_map/convert_element_type | solution.py:111
  (105 shorter events, 22.4 us)
Async XLA Ops:
  7.2 41.4 %copy-start = (f32[512,512]{1,0:T(8,128)S(1)}, f32[512,512]{1,0:T(8,128)}, u32[]{:S(2)}) copy-start(f32[512,512]{1,0:T(8,128)} %param.10) | copy-start | bytes 3145732
  7.2 103.0 %all-gather.3.cloned.1.call-start = ((), (), s32[]{:S(2)}) async-start(), calls=%async_computation | async-start | bytes 4718592 | tf_op jit(solution)/shard_map/all_gather | solution.py:64
  9.2 12.1 %collective-permute-start.21 = (bf16[2,2,2,32,512]{4,3,2,1,0:T(8,128)(2,1)S(1)}, bf16[2,2,2,32,512]{4,3,2,1,0:T(8,128)(2,1)S(1)}, u32[]{:S(2)}, u32[]{:S(2)}) collective-permute-start(bf16[2,2,2,32,512]{4,3,2,1,0:T(8,128)(2,1)S(1)} %dynamic-slice_bitcast_fusion.1), channel_id=1, source_target_pairs={{0,16},{16,0},{32,48},{48,32},{64,80},{80,64},{96,112},{112,96},{1... | collective-permute-start | bytes 786440 | tf_op jit(solution)/shard_map/ppermute | solution.py:38
  18.7 2.5 %collective-permute-start.10 = (f32[8,128]{1,0:T(8,128)S(1)}, f32[8,128]{1,0:T(8,128)S(1)}, u32[]{:S(2)}, u32[]{:S(2)}) collective-permute-start(f32[8,128]{1,0:T(8,128)S(1)} %broadcast_in_dim.6), channel_id=1, source_target_pairs={{0,8},{1,9},{2,10},{3,11},{4,12},{5,13},{6,14},{7,15},{8,0},{9,1},... | collective-permute-start | bytes 12296 | tf_op jit(solution)/shard_map/ppermute | solution.py:79
  18.8 31.2 %collective-permute-start.1 = (bf16[384,512]{1,0:T(8,128)(2,1)S(1)}, bf16[384,512]{1,0:T(8,128)(2,1)S(1)}, u32[]{:S(2)}, u32[]{:S(2)}) collective-permute-start(bf16[384,512]{1,0:T(8,128)(2,1)S(1)} %bitcast.135), channel_id=1, source_target_pairs={{0,8},{1,9},{2,10},{3,11},{4,12},{5,13},{6,14},{7,15},{8,0},{9,1},... | collective-permute-start | bytes 1179656 | tf_op jit(solution)/shard_map/ppermute | solution.py:66
  21.3 6.0 %collective-permute-start.11 = (f32[8,128]{1,0:T(8,128)S(1)}, f32[8,128]{1,0:T(8,128)S(1)}, u32[]{:S(2)}, u32[]{:S(2)}) collective-permute-start(f32[8,128]{1,0:T(8,128)S(1)} %broadcast_maximum_fusion), channel_id=1, source_target_pairs={{0,1},{1,0},{2,3},{3,2},{4,5},{5,4},{6,7},{7,6},{8,9},{9,8},{10,11... | collective-permute-start | bytes 12296 | tf_op jit(solution)/shard_map/ppermute | solution.py:79
  21.4 8.9 %collective-permute-start.22 = (f32[2,2,32,512]{3,2,1,0:T(8,128)S(1)}, f32[2,2,32,512]{3,2,1,0:T(8,128)}, u32[]{:S(2)}, u32[]{:S(2)}) collective-permute-start(f32[2,2,32,512]{3,2,1,0:T(8,128)S(1)} %dynamic-slice_bitcast_fusion), channel_id=1, source_target_pairs={{0,32},{16,48},{32,0},{48,16},{64,96},{80,112},{96,64},{112,80},{1... | collective-permute-start | bytes 786440 | tf_op jit(solution)/shard_map/ppermute | solution.py:38
  26.0 24.3 %collective-permute-start = (bf16[384,512]{1,0:T(8,128)(2,1)}, bf16[384,512]{1,0:T(8,128)(2,1)S(1)}, u32[]{:S(2)}, u32[]{:S(2)}) collective-permute-start(bf16[384,512]{1,0:T(8,128)(2,1)} %get-tuple-element.22), channel_id=1, source_target_pairs={{0,8},{1,9},{2,10},{3,11},{4,12},{5,13},{6,14},{7,15},{8,0},{9,1},... | collective-permute-start | bytes 1179656 | tf_op jit(solution)/shard_map/ppermute | solution.py:74
  27.3 14.1 %collective-permute-start.12 = (f32[8,128]{1,0:T(8,128)S(1)}, f32[8,128]{1,0:T(8,128)S(1)}, u32[]{:S(2)}, u32[]{:S(2)}) collective-permute-start(f32[8,128]{1,0:T(8,128)S(1)} %fusion.96), channel_id=1, source_target_pairs={{0,2},{1,3},{2,0},{3,1},{4,6},{5,7},{6,4},{7,5},{8,10},{9,11},{10,... | collective-permute-start | bytes 12296 | tf_op jit(solution)/shard_map/ppermute | solution.py:79
  31.3 20.3 %copy-start.13 = (f32[512,32]{0,1:T(8,128)S(1)}, f32[512,32]{0,1:T(8,128)}, u32[]{:S(2)}) copy-start(f32[512,32]{0,1:T(8,128)} %param.11) | copy-start | bytes 196612
  31.3 14.4 %collective-permute-start.23 = (f32[2,32,512]{2,1,0:T(8,128)S(1)}, f32[2,32,512]{2,1,0:T(8,128)S(1)}, u32[]{:S(2)}, u32[]{:S(2)}) collective-permute-start(f32[2,32,512]{2,1,0:T(8,128)S(1)} %dynamic-slice_bitcast_fusion.2), channel_id=1, source_target_pairs={{0,64},{16,80},{32,96},{48,112},{64,0},{80,16},{96,32},{112,48},{1... | collective-permute-start | bytes 393224 | tf_op jit(solution)/shard_map/ppermute | solution.py:38
  41.4 7.3 %collective-permute-start.13 = (f32[8,128]{1,0:T(8,128)S(1)}, f32[8,128]{1,0:T(8,128)S(1)}, u32[]{:S(2)}, u32[]{:S(2)}) collective-permute-start(f32[8,128]{1,0:T(8,128)S(1)} %max.18), channel_id=1, source_target_pairs={{0,4},{1,5},{2,6},{3,7},{4,0},{5,1},{6,2},{7,3},{8,12},{9,13},{10,... | collective-permute-start | bytes 12296 | tf_op jit(solution)/shard_map/ppermute | solution.py:79
  45.8 5.8 %collective-permute-start.24 = (f32[32,512]{1,0:T(8,128)S(1)}, f32[32,512]{1,0:T(8,128)S(1)}, u32[]{:S(2)}, u32[]{:S(2)}) collective-permute-start(f32[32,512]{1,0:T(8,128)S(1)} %dynamic-slice_bitcast_fusion.3), channel_id=1, source_target_pairs={{0,128},{16,144},{32,160},{48,176},{64,192},{80,208},{96,224},{112... | collective-permute-start | bytes 196616 | tf_op jit(solution)/shard_map/ppermute | solution.py:38
  50.0 18.6 %collective-permute-start.2 = (bf16[384,512]{1,0:T(8,128)(2,1)}, bf16[384,512]{1,0:T(8,128)(2,1)S(1)}, u32[]{:S(2)}, u32[]{:S(2)}) collective-permute-start(bf16[384,512]{1,0:T(8,128)(2,1)} %get-tuple-element.11), channel_id=1, source_target_pairs={{0,8},{1,9},{2,10},{3,11},{4,12},{5,13},{6,14},{7,15},{8,0},{9,1},... | collective-permute-start | bytes 1179656 | tf_op jit(solution)/shard_map/ppermute | solution.py:74
  50.3 19.7 %collective-permute-start.3 = (bf16[384,512]{1,0:T(8,128)(2,1)}, bf16[384,512]{1,0:T(8,128)(2,1)S(1)}, u32[]{:S(2)}, u32[]{:S(2)}) collective-permute-start(bf16[384,512]{1,0:T(8,128)(2,1)} %get-tuple-element.12), channel_id=1, source_target_pairs={{0,8},{1,9},{2,10},{3,11},{4,12},{5,13},{6,14},{7,15},{8,0},{9,1},... | collective-permute-start | bytes 1179656 | tf_op jit(solution)/shard_map/ppermute | solution.py:74
  52.2 15.8 %collective-permute-start.25 = (f32[32,512]{1,0:T(8,128)S(1)}, f32[32,512]{1,0:T(8,128)S(1)}, u32[]{:S(2)}, u32[]{:S(2)}) collective-permute-start(f32[32,512]{1,0:T(8,128)S(1)} %get-tuple-element.35), channel_id=1, source_target_pairs={{0,128},{16,144},{32,160},{48,176},{64,192},{80,208},{96,224},{112... | collective-permute-start | bytes 196616 | tf_op jit(solution)/shard_map/ppermute | solution.py:44
  55.9 22.0 %collective-permute-start.14 = (f16[512,512]{1,0:T(8,128)(2,1)S(1)}, f16[512,512]{1,0:T(8,128)(2,1)S(1)}, u32[]{:S(2)}, u32[]{:S(2)}) collective-permute-start(f16[512,512]{1,0:T(8,128)(2,1)S(1)} %fusion.22), channel_id=1, source_target_pairs={{0,1},{1,2},{2,3},{3,4},{4,5},{5,6},{6,7},{7,0},{8,9},{9,10},{10,1... | collective-permute-start | bytes 1572872 | tf_op jit(solution)/shard_map/ppermute | solution.py:96
  68.1 6.7 %collective-permute-start.26 = (f32[2,32,512]{2,1,0:T(8,128)S(1)}, f32[2,32,512]{2,1,0:T(8,128)S(1)}, u32[]{:S(2)}, u32[]{:S(2)}) collective-permute-start(f32[2,32,512]{2,1,0:T(8,128)S(1)} %pad_maximum_fusion.3), channel_id=1, source_target_pairs={{0,64},{16,80},{32,96},{48,112},{64,0},{80,16},{96,32},{112,48},{1... | collective-permute-start | bytes 393224 | tf_op jit(solution)/shard_map/ppermute | solution.py:44
  68.6 19.8 %collective-permute-start.4 = (bf16[384,512]{1,0:T(8,128)(2,1)}, bf16[384,512]{1,0:T(8,128)(2,1)S(1)}, u32[]{:S(2)}, u32[]{:S(2)}) collective-permute-start(bf16[384,512]{1,0:T(8,128)(2,1)} %get-tuple-element.13), channel_id=1, source_target_pairs={{0,8},{1,9},{2,10},{3,11},{4,12},{5,13},{6,14},{7,15},{8,0},{9,1},... | collective-permute-start | bytes 1179656 | tf_op jit(solution)/shard_map/ppermute | solution.py:74
  70.0 18.5 %collective-permute-start.5 = (bf16[384,512]{1,0:T(8,128)(2,1)}, bf16[384,512]{1,0:T(8,128)(2,1)S(1)}, u32[]{:S(2)}, u32[]{:S(2)}) collective-permute-start(bf16[384,512]{1,0:T(8,128)(2,1)} %get-tuple-element.14), channel_id=1, source_target_pairs={{0,8},{1,9},{2,10},{3,11},{4,12},{5,13},{6,14},{7,15},{8,0},{9,1},... | collective-permute-start | bytes 1179656 | tf_op jit(solution)/shard_map/ppermute | solution.py:74
  72.1 17.9 %collective-permute-start.18 = (f16[512,512]{1,0:T(8,128)(2,1)S(1)}, f16[512,512]{1,0:T(8,128)(2,1)S(1)}, u32[]{:S(2)}, u32[]{:S(2)}) collective-permute-start(f16[512,512]{1,0:T(8,128)(2,1)S(1)} %fusion.23), channel_id=1, source_target_pairs={{0,7},{1,0},{2,1},{3,2},{4,3},{5,4},{6,5},{7,6},{8,15},{9,8},{10,9... | collective-permute-start | bytes 1572872 | tf_op jit(solution)/shard_map/ppermute | solution.py:100
  74.9 5.6 %collective-permute-start.27 = (f32[2,2,32,512]{3,2,1,0:T(8,128)S(1)}, f32[2,2,32,512]{3,2,1,0:T(8,128)S(1)}, u32[]{:S(2)}, u32[]{:S(2)}) collective-permute-start(f32[2,2,32,512]{3,2,1,0:T(8,128)S(1)} %pad_maximum_fusion.2), channel_id=1, source_target_pairs={{0,32},{16,48},{32,0},{48,16},{64,96},{80,112},{96,64},{112,80},{1... | collective-permute-start | bytes 786440 | tf_op jit(solution)/shard_map/ppermute | solution.py:44
  79.6 13.8 %collective-permute-start.15 = (f16[512,512]{1,0:T(8,128)(2,1)S(1)}, f16[512,512]{1,0:T(8,128)(2,1)S(1)}, u32[]{:S(2)}, u32[]{:S(2)}) collective-permute-start(f16[512,512]{1,0:T(8,128)(2,1)S(1)} %fusion.32), channel_id=1, source_target_pairs={{0,1},{1,2},{2,3},{3,4},{4,5},{5,6},{6,7},{7,0},{8,9},{9,10},{10,1... | collective-permute-start | bytes 1572872 | tf_op jit(solution)/shard_map/ppermute | solution.py:96
  80.6 18.7 %collective-permute-start.28 = (f32[2,2,2,32,512]{4,3,2,1,0:T(8,128)S(1)}, f32[2,2,2,32,512]{4,3,2,1,0:T(8,128)S(1)}, u32[]{:S(2)}, u32[]{:S(2)}) collective-permute-start(f32[2,2,2,32,512]{4,3,2,1,0:T(8,128)S(1)} %pad_maximum_fusion.1), channel_id=1, source_target_pairs={{0,16},{16,0},{32,48},{48,32},{64,80},{80,64},{96,112},{112,96},{1... | collective-permute-start | bytes 1572872 | tf_op jit(solution)/shard_map/ppermute | solution.py:44
  88.5 10.7 %collective-permute-start.6 = (bf16[384,512]{1,0:T(8,128)(2,1)S(1)}, bf16[384,512]{1,0:T(8,128)(2,1)S(1)}, u32[]{:S(2)}, u32[]{:S(2)}) collective-permute-start(bf16[384,512]{1,0:T(8,128)(2,1)S(1)} %get-tuple-element.15), channel_id=1, source_target_pairs={{0,8},{1,9},{2,10},{3,11},{4,12},{5,13},{6,14},{7,15},{8,0},{9,1},... | collective-permute-start | bytes 1179656 | tf_op jit(solution)/shard_map/ppermute | solution.py:74
  88.5 20.3 %collective-permute-start.7 = (bf16[384,512]{1,0:T(8,128)(2,1)}, bf16[384,512]{1,0:T(8,128)(2,1)S(1)}, u32[]{:S(2)}, u32[]{:S(2)}) collective-permute-start(bf16[384,512]{1,0:T(8,128)(2,1)} %get-tuple-element.16), channel_id=1, source_target_pairs={{0,8},{1,9},{2,10},{3,11},{4,12},{5,13},{6,14},{7,15},{8,0},{9,1},... | collective-permute-start | bytes 1179656 | tf_op jit(solution)/shard_map/ppermute | solution.py:74
  90.5 13.6 %collective-permute-start.19 = (f16[512,512]{1,0:T(8,128)(2,1)S(1)}, f16[512,512]{1,0:T(8,128)(2,1)S(1)}, u32[]{:S(2)}, u32[]{:S(2)}) collective-permute-start(f16[512,512]{1,0:T(8,128)(2,1)S(1)} %fusion.34), channel_id=1, source_target_pairs={{0,7},{1,0},{2,1},{3,2},{4,3},{5,4},{6,5},{7,6},{8,15},{9,8},{10,9... | collective-permute-start | bytes 1572872 | tf_op jit(solution)/shard_map/ppermute | solution.py:100
  94.0 14.8 %collective-permute-start.16 = (f16[512,512]{1,0:T(8,128)(2,1)S(1)}, f16[512,512]{1,0:T(8,128)(2,1)S(1)}, u32[]{:S(2)}, u32[]{:S(2)}) collective-permute-start(f16[512,512]{1,0:T(8,128)(2,1)S(1)} %fusion.31), channel_id=1, source_target_pairs={{0,1},{1,2},{2,3},{3,4},{4,5},{5,6},{6,7},{7,0},{8,9},{9,10},{10,1... | collective-permute-start | bytes 1572872 | tf_op jit(solution)/shard_map/ppermute | solution.py:96
  99.2 18.0 %collective-permute-start.8 = (bf16[384,512]{1,0:T(8,128)(2,1)}, bf16[384,512]{1,0:T(8,128)(2,1)S(1)}, u32[]{:S(2)}, u32[]{:S(2)}) collective-permute-start(bf16[384,512]{1,0:T(8,128)(2,1)} %get-tuple-element.17), channel_id=1, source_target_pairs={{0,8},{1,9},{2,10},{3,11},{4,12},{5,13},{6,14},{7,15},{8,0},{9,1},... | collective-permute-start | bytes 1179656 | tf_op jit(solution)/shard_map/ppermute | solution.py:74
  105.4 15.3 %collective-permute-start.20 = (f16[512,512]{1,0:T(8,128)(2,1)}, f16[512,512]{1,0:T(8,128)(2,1)}, u32[]{:S(2)}, u32[]{:S(2)}) collective-permute-start(f16[512,512]{1,0:T(8,128)(2,1)} %fusion.33), channel_id=1, source_target_pairs={{0,7},{1,0},{2,1},{3,2},{4,3},{5,4},{6,5},{7,6},{8,15},{9,8},{10,9... | collective-permute-start | bytes 1572872 | tf_op jit(solution)/shard_map/ppermute | solution.py:100
  110.1 13.2 %collective-permute-start.17 = (f16[512,512]{1,0:T(8,128)(2,1)}, f16[512,512]{1,0:T(8,128)(2,1)}, u32[]{:S(2)}, u32[]{:S(2)}) collective-permute-start(f16[512,512]{1,0:T(8,128)(2,1)} %fusion.30), channel_id=1, source_target_pairs={{0,1},{1,2},{2,3},{3,4},{4,5},{5,6},{6,7},{7,0},{8,9},{9,10},{10,1... | collective-permute-start | bytes 1572872 | tf_op jit(solution)/shard_map/ppermute | solution.py:96
  119.0 17.6 %collective-permute-start.9 = (f32[384,512]{1,0:T(8,128)}, f32[384,512]{1,0:T(8,128)}, u32[]{:S(2)}, u32[]{:S(2)}) collective-permute-start(f32[384,512]{1,0:T(8,128)} %fusion.29), channel_id=1, source_target_pairs={{0,8},{1,9},{2,10},{3,11},{4,12},{5,13},{6,14},{7,15},{8,0},{9,1},... | collective-permute-start | bytes 2359304 | tf_op jit(solution)/shard_map/ppermute | solution.py:110
  (12 other events, 116.2 us)
Sparse Core Ops, SparseCore 0:
  9.8 65.1 all-gather.2

commit v2 on v0

v2 whole, which is shorter than its diff:
```python
import jax
import jax.numpy as jnp
from jax import lax
from jax.sharding import PartitionSpec as P

outer_rate = 0.7
outer_mu = 0.9

Z = 8
PAIR = [(i, (i + Z) % (2 * Z)) for i in range(2 * Z)]
UP = [(i, i // Z * Z + (i + 1) % Z) for i in range(2 * Z)]
DOWN = [(i, i // Z * Z + (i - 1) % Z) for i in range(2 * Z)]
ORDER = (4, -3, 3, -2, 2, -1, 1, 0)
f32 = jnp.float32
LIMIT = 6144 * 6 * 0.0796
PACK = 65000.0**2 / LIMIT


def coded(x):
    root = jnp.sqrt(jnp.abs(x) * PACK)
    return jnp.where(x < 0, -root, root).astype(jnp.float16)


def decoded(x):
    x = x.astype(f32)
    return x * jnp.abs(x) * (1 / PACK)


def xor(bit):
    return [(i, i ^ bit) for i in range(16)]


def after(x, *deps):
    return lax.optimization_barrier((x, *deps))[0]


def pick(a, i, axis):
    return lax.dynamic_index_in_dim(a, i, axis, keepdims=False)


class Order:
    def __init__(self):
        self.last = ()

    def gate(self, *xs):
        if not self.last:
            return xs if len(xs) > 1 else xs[0]
        out = lax.optimization_barrier((*xs, *self.last))
        return out[: len(xs)] if len(xs) > 1 else out[0]

    def done(self, *xs):
        self.last = xs


def per_device(
    normed, value_weight, value_cotangent, local_fragment, global_fragment, outer_momentum
):
    micro_count, tok_rows, model_width = normed.shape
    kv = value_cotangent.shape[2]
    tokens = micro_count * tok_rows
    half = model_width // 2
    chunk = half // Z
    n = normed.reshape(tokens, model_width)
    c = value_cotangent.reshape(tokens, kv)
    fsdp = lax.axis_index("fsdp").astype(jnp.uint32)
    yl, z = fsdp >> 3, fsdp & 7
    spots = [((z + (o & 7)) & 7) * chunk for o in ORDER]
    order = Order()

    def cut(s, side):
        return lax.dynamic_slice_in_dim(n, side * half + spots[s], chunk, 1)

    def tn(a, b):
        return lax.dot_general(a, b, (((0,), (0,)), ((), ())), preferred_element_type=f32)

    def over_y(x):
        return lax.ppermute(x, "fsdp", PAIR)

    island = lax.axis_index("island").astype(jnp.uint32)
    bits = [(island >> b) & 1 for b in range(4)]
    cols = outer_momentum.shape[1]
    rows = global_fragment.shape[0]

    def fold_send(part, b):
        return lax.ppermute(pick(part, 1 - bits[b], 3 - b), "island", xor(1 << b))

    def fold(part, got, b):
        return pick(part, bits[b], 3 - b).astype(f32) + got.astype(f32)

    def spread_send(full, b):
        return lax.ppermute(full, "island", xor(1 << b))

    def spread(full, got, b):
        low = bits[b] == 0
        return jnp.stack([jnp.where(low, full, got), jnp.where(low, got, full)], 3 - b)

    c_p = over_y(c)
    w = {0: value_weight[0]}

    def w_hop(way, h):
        w[-way * h] = lax.ppermute(w[-way * (h - 1)], "fsdp", UP if way > 0 else DOWN)

    def next_w(way, h):
        w[-way * h] = order.gate(w[-way * h])
        w_hop(way, h + 1)
        order.done(w[-way * h])

    send = [cut(s, 1 - yl) for s in range(Z)]
    order.done(*send)
    k = [None] * Z
    k[0] = over_y(send[0])
    w[0] = order.gate(w[0])
    w_hop(1, 1)
    w_hop(-1, 1)
    own = [None] * Z

    def own_dots(*steps):
        cc = order.gate(c)
        for s in steps:
            own[s] = tn(ours[s], cc)
        order.done(*[own[s] for s in steps])

    full = None

    def fold_step(b):
        nonlocal part, sent
        sent, part = order.gate(sent, part)
        part = fold(part, sent, b)
        if b < 3:
            sent = fold_send(part, b + 1)
        order.done(part)

    def spread_step(b):
        nonlocal full, sent
        sent, full = order.gate(sent, full)
        full = spread(full, sent, b)
        if b > 0:
            sent = spread_send(full, b - 1)
        order.done(full)

    carry = {1: None, -1: None}

    def ring(s):
        got, mine, cc = order.gate(k[s], own[s], c_p)
        g = mine + tn(got, cc)
        o = ORDER[s]
        if o == 0:
            g = g + decoded(carry[1]) + decoded(carry[-1])
            order.done(g)
            return g
        way = 1 if o > 0 else -1
        if carry[way] is not None:
            g = g + decoded(carry[way])
        g = coded(g)
        order.done(g)
        carry[way] = lax.ppermute(g, "fsdp", UP if way > 0 else DOWN)

    def next_chunk(s):
        if s + 3 < Z:
            k[s], send[s + 3] = order.gate(k[s], send[s + 3])
            k[s + 3] = over_y(send[s + 3])
            order.done(k[s], send[s + 3])

    def start_chunk(s, *deps):
        out = order.gate(send[s], *deps)
        send[s] = out[0] if deps else out
        k[s] = over_y(send[s])
        order.done(send[s], *out[1:] if deps else ())

    def theirs(steps, so_far):
        return products(k, steps, so_far)

    def products(blocks, steps, so_far):
        gated = order.gate(*[blocks[s] for s in steps], *[w[ORDER[s]] for s in steps])
        for got, rows_w in zip(gated[: len(steps)], gated[len(steps) :]):
            d = jnp.dot(got, rows_w, preferred_element_type=f32)
            so_far = d if so_far is None else so_far + d
        order.done(so_far)
        return so_far

    local = order.gate(local_fragment[0])
    part = local.T.reshape(2, 2, 2, 2, cols, rows)
    sent = fold_send(part, 0)
    order.done(part)
    n, c_p = order.gate(n, c_p)
    ours = [cut(s, yl) for s in range(Z)]
    order.done(*ours)
    start_chunk(1)
    next_w(1, 1)
    next_w(-1, 1)
    own_dots(0)
    start_chunk(2)
    ring(0)
    fold_step(0)
    own_dots(1, 2)
    next_chunk(0)
    next_chunk(1)
    ring(1)
    next_w(1, 2)
    next_w(-1, 2)
    fold_step(1)
    next_chunk(2)
    ring(2)
    own_dots(3)
    next_chunk(3)
    ring(3)
    fold_step(2)
    next_w(-1, 3)
    next_chunk(4)
    partner = theirs((2, 3, 4), None)
    own_dots(4)
    ring(4)
    own_dots(5)
    ring(5)
    fold_step(3)
    mine = lax.dynamic_slice_in_dim(global_fragment.T, island * cols, cols, 0)
    pseudo = mine - part / 16
    momentum = outer_mu * outer_momentum.T + pseudo
    full = mine - outer_rate * (pseudo + outer_mu * momentum)
    sent = spread_send(full, 3)
    order.done(full)
    own_dots(6)
    partner = theirs((1, 5), partner)
    ring(6)
    partner = theirs((0, 6), partner)
    partner = theirs((7,), partner)
    back = over_y(partner)
    spread_step(3)
    forward = products(ours, range(Z), None)
    spread_step(2)
    own_dots(7)
    spread_step(1)
    value_grad = ring(7)[None]
    spread_step(0)
    new_global = full.reshape(-1, rows).T
    order.done(new_global)
    back, forward = order.gate(back, forward)
    projected = (forward + back).astype(jnp.bfloat16).reshape(micro_count, tok_rows, kv)
    return (projected, value_grad, new_global, momentum.T)


def solution(mesh):
    placed = (
        P(None, ("island", "fsdp"), None),
        P("island", "fsdp", None),
        P(None, ("island", "fsdp"), None),
        P("island", "fsdp", None),
        P("fsdp", None),
        P("fsdp", "island"),
    )
    return jax.shard_map(
        per_device,
        mesh=mesh,
        in_specs=placed,
        out_specs=(
            P(None, ("island", "fsdp"), None),
            P("island", "fsdp", None),
            P("fsdp", None),
            P("fsdp", "island"),
        ),
        check_vma=False,
    )
```

time: 511 us -> 115 us (0.23)
  waiting for transfers between devices: 467 us -> 24.4 us
  starting transfers between devices: 0.16 us -> 49.1 us
  between operations: 13.8 us -> 1.2 us
  local copies, waits for them, and re-layouts: 4.18 us -> 12.8 us
    reduce_scatter x1 -> x0, waiting for transfers between devices: 177 us -> none  [per_device(): lax.psum_scatter(lax.dot_general(columns, flat_cots, (((0,), (0,)), ((),...]
    psum x1 -> x0, waiting for transfers between devices: 149 us -> none  [per_device(): pseudo = lax.psum(own_delta, 'island') / islands]
    all_gather x2 -> x0, waiting for transfers between devices: 140 us -> none  [the longest x1 98.5 us: per_device(): lax.all_gather(value_weight[0], 'fsdp', axis=0, tiled=True)]
    ppermute x0 -> x32, starting transfers between devices: none -> 49.1 us  [the longest x7 13.6 us: w_hop(): lax.ppermute(w[-way * (h - 1)], 'fsdp', UP if way > 0 else DOWN)]
    ppermute x0 -> x32, waiting for transfers between devices: none -> 24.4 us  [the longest x4 6.41 us: fold_send(): return lax.ppermute(pick(part, 1 - bits[b], 3 - b), 'island', xor(1 << b))]
    dynamic_slice x0 -> x2, local copies, waits for them, and re-layouts: none -> 5.76 us  [cut(): return lax.dynamic_slice_in_dim(n, side * half + spots[s], chunk, 1)]
    convert_element_type x0 -> x6, other arithmetic: none -> 5.39 us  [the longest x5 3.16 us: coded(): return jnp.where(x < 0, -root, root).astype(jnp.float16)]
    dot_general x2 -> x32, matrix products: 20.4 us -> 18.2 us  [the longest x16 9.38 us: tn(): lax.dot_general(a, b, (((0,), (0,)), ((), ())), preferred_element_type=f32)]
  transfers between devices with their start and end apart: 4 -> 32, of which waited for: 4 -> 9; matrix products, arithmetic and copies ran while one was open for 5% -> 33% of each run, Pallas kernels for 0% -> 0%
where the time goes in v2:
time: 115 us
  starting transfers between devices  49.1 us (43%)
  waiting for transfers between devices  24.4 us (21%)
  matrix products  18.2 us (16%)
  local copies, waits for them, and re-layouts  12.8 us (11%)
  other arithmetic  8.85 us (8%)
  between operations  1.2 us (1%)
    ppermute x7, starting transfers between devices, w_hop(): lax.ppermute(w[-way * (h - 1)], 'fsdp', UP if way > 0 else DOWN)  13.6 us
    ppermute x4, starting transfers between devices, spread_send(): return lax.ppermute(full, 'island', xor(1 << b))  11 us
    dot_general x16, matrix products, tn(): lax.dot_general(a, b, (((0,), (0,)), ((), ())), preferred_element_type=f32)  9.38 us
    ppermute x7, starting transfers between devices, ring(): carry[way] = lax.ppermute(g, 'fsdp', UP if way > 0 else DOWN)  9.33 us
    dot_general x16, matrix products, products(): d = jnp.dot(got, rows_w, preferred_element_type=f32)  8.86 us
    ppermute x4, starting transfers between devices, fold_send(): return lax.ppermute(pick(part, 1 - bits[b], 3 - b), 'island', xor(1 << b))  7.97 us
    ppermute x10, starting transfers between devices, over_y(): return lax.ppermute(x, 'fsdp', PAIR)  7.09 us
    ppermute x4, waiting for transfers between devices, fold_send(): return lax.ppermute(pick(part, 1 - bits[b], 3 - b), 'island', xor(1 << b))  6.41 us
  transfers between devices with their start and end apart: 32, of which 9 were waited for; matrix products, arithmetic and copies ran while one was open for 33% of the time, Pallas kernels for 0%

profile of v2, /device:TPU:1, one launch (start us, length us, event | category | flops | bytes accessed | tf_op | source)
XLA Modules:
  0.0 114.5 jit_solution(3757433391036126508)
XLA Ops:
  0.7 2.2 %collective-permute-start = (bf16[384,512]{1,0:T(8,128)(2,1)}, bf16[384,512]{1,0:T(8,128)(2,1)S(1)}, u32[]{:S(2)}, u32[]{:S(2)}) collective-permute-start(bf16[384,512]{1,0:T(8,128)(2,1)} %bitcast.138), channel_id=1, source_target_pairs={{0,8},{1,9},{2,10},{3,11},{4,12},{5,13},{6,14},{7,15},{8,0},{9,1},... | collective-permute-start | bytes 1179656 | tf_op jit(solution)/shard_map/ppermute | solution.py:77
  2.9 3.6 %constant_dynamic-slice_fusion.9 = (bf16[384,512]{1,0:T(8,128)(2,1)}, bf16[384,512]{1,0:T(8,128)(2,1)}, bf16[384,512]{1,0:T(8,128)(2,1)}, bf16[384,512]{1,0:T(8,...) fusion(bf16[384,8192]{1,0:T(8,128)(2,1)} %bitcast.147, ...), kind=kLoop, calls=%fused_computation.88 | loop fusion | bytes 6291488 | tf_op jit(solution)/shard_map/dynamic_slice | solution.py:71
  6.5 1.7 %collective-permute-start.2 = (bf16[512,512]{1,0:T(8,128)(2,1)S(1)}, bf16[512,512]{1,0:T(8,128)(2,1)S(1)}, u32[]{:S(2)}, u32[]{:S(2)}) collective-permute-start(bf16[512,512]{1,0:T(8,128)(2,1)S(1)} %bitcast.150), channel_id=1, source_target_pairs={{0,1},{1,2},{2,3},{3,4},{4,5},{5,6},{6,7},{7,0},{8,9},{9,10},{10,1... | collective-permute-start | bytes 1572872 | tf_op jit(solution)/shard_map/ppermute | solution.py:101
  8.2 4.0 %collective-permute-start.1 = (bf16[512,512]{1,0:T(8,128)(2,1)S(1)}, bf16[512,512]{1,0:T(8,128)(2,1)S(1)}, u32[]{:S(2)}, u32[]{:S(2)}) collective-permute-start(bf16[512,512]{1,0:T(8,128)(2,1)S(1)} %bitcast.151), channel_id=1, source_target_pairs={{0,7},{1,0},{2,1},{3,2},{4,3},{5,4},{6,5},{7,6},{8,15},{9,8},{10,9... | collective-permute-start | bytes 1572872 | tf_op jit(solution)/shard_map/ppermute | solution.py:101
  12.4 2.0 %copy.11 = bf16[1,512,512]{1,2,0:T(8,128)(2,1)} copy(bf16[1,512,512]{2,1,0:T(8,128)(2,1)} %param.9) | data formatting | bytes 1048576 | tf_op args[3]
  14.5 1.7 %dynamic-slice_bitcast_fusion.1 = bf16[2,2,2,32,512]{4,3,2,1,0:T(8,128)(2,1)} fusion(bf16[2,2,2,2,32,512]{5,4,3,2,1,0:T(8,128)(2,1)} %bitcast.154, u32[]{:T(128)S(6)} %sub.29), kind=kLoop, calls=%fused_computation.64 | loop fusion | bytes 524292 | tf_op jit(solution)/shard_map/jit(dynamic_index_in_dim)/squeeze | solution.py:38
  16.2 1.4 %collective-permute-start.4 = (bf16[2,2,2,32,512]{4,3,2,1,0:T(8,128)(2,1)}, bf16[2,2,2,32,512]{4,3,2,1,0:T(8,128)(2,1)}, u32[]{:S(2)}, u32[]{:S(2)}) collective-permute-start(bf16[2,2,2,32,512]{4,3,2,1,0:T(8,128)(2,1)} %dynamic-slice_bitcast_fusion.1), channel_id=1, source_target_pairs={{0,16},{16,0},{32,48},{48,32},{64,80},{80,64},{96,112},{112,96},{1... | collective-permute-start | bytes 786440 | tf_op jit(solution)/shard_map/ppermute | solution.py:85
  19.5 2.1 %constant_dynamic-slice_fusion.1 = (bf16[384,512]{1,0:T(8,128)(2,1)S(1)}, bf16[384,512]{1,0:T(8,128)(2,1)S(1)}, bf16[384,512]{1,0:T(8,128)(2,1)S(1)}, bf16[384,5...) fusion(bf16[384,8192]{1,0:T(8,128)(2,1)} %bitcast.148, ...), kind=kLoop, calls=%fused_computation.80 | loop fusion | bytes 6291488 | tf_op jit(solution)/shard_map/dynamic_slice | solution.py:71
  21.7 1.4 %collective-permute-start.9 = (bf16[384,512]{1,0:T(8,128)(2,1)S(1)}, bf16[384,512]{1,0:T(8,128)(2,1)S(1)}, u32[]{:S(2)}, u32[]{:S(2)}) collective-permute-start(bf16[384,512]{1,0:T(8,128)(2,1)S(1)} %copy-done.11), channel_id=1, source_target_pairs={{0,8},{1,9},{2,10},{3,11},{4,12},{5,13},{6,14},{7,15},{8,0},{9,1},... | collective-permute-start | bytes 1179656 | tf_op jit(solution)/shard_map/ppermute | solution.py:77
  23.4 2.7 %collective-permute-start.7 = (bf16[512,512]{1,0:T(8,128)(2,1)S(1)}, bf16[512,512]{1,0:T(8,128)(2,1)S(1)}, u32[]{:S(2)}, u32[]{:S(2)}) collective-permute-start(bf16[512,512]{1,0:T(8,128)(2,1)S(1)} %collective-permute-done.1), channel_id=1, source_target_pairs={{0,7},{1,0},{2,1},{3,2},{4,3},{5,4},{6,5},{7,6},{8,15},{9,8},{10,9... | collective-permute-start | bytes 1572872 | tf_op jit(solution)/shard_map/ppermute | solution.py:101
  26.6 1.5 %fusion.33 = f32[512,512]{1,0:T(8,128)S(1)} fusion(bf16[384,512]{1,0:T(8,128)(2,1)} %collective-permute-done.5, bf16[384,512]{1,0:T(8,128)(2,1)S(1)} %collective-permute-done), kind=kOutput, calls=%fused_computation.97 | convolution fusion | flops 201326592 | bytes 1835008 | tf_op jit(solution)/shard_map/dot_general | solution.py:74
  31.1 1.4 %collective-permute-done.9 = bf16[384,512]{1,0:T(8,128)(2,1)S(1)} collective-permute-done((bf16[384,512]{1,0:T(8,128)(2,1)S(1)}, bf16[384,512]{1,0:T(8,128)(2,1)S(1)}, u32[]{:S(2)}, u32[]{:S(2)}) %collective-permute-start.9) | collective-permute-done | bytes 393248 | tf_op jit(solution)/shard_map/ppermute | solution.py:77
  34.6 1.9 %collective-permute-done.8 = bf16[512,512]{1,0:T(8,128)(2,1)S(1)} collective-permute-done((bf16[512,512]{1,0:T(8,128)(2,1)S(1)}, bf16[512,512]{1,0:T(8,128)(2,1)S(1)}, u32[]{:S(2)}, u32[]{:S(2)}) %collective-permute-start.8) | collective-permute-done | bytes 524320 | tf_op jit(solution)/shard_map/ppermute | solution.py:101
  37.0 2.0 %collective-permute-start.15 = (f16[512,512]{1,0:T(8,128)(2,1)S(1)}, f16[512,512]{1,0:T(8,128)(2,1)S(1)}, u32[]{:S(2)}, u32[]{:S(2)}) collective-permute-start(f16[512,512]{1,0:T(8,128)(2,1)S(1)} %fusion.9), channel_id=1, source_target_pairs={{0,7},{1,0},{2,1},{3,2},{4,3},{5,4},{6,5},{7,6},{8,15},{9,8},{10,9... | collective-permute-start | bytes 1572872 | tf_op jit(solution)/shard_map/ppermute | solution.py:156
  40.5 2.3 %collective-permute-start.13 = (bf16[512,512]{1,0:T(8,128)(2,1)S(1)}, bf16[512,512]{1,0:T(8,128)(2,1)S(1)}, u32[]{:S(2)}, u32[]{:S(2)}) collective-permute-start(bf16[512,512]{1,0:T(8,128)(2,1)S(1)} %collective-permute-done.7), channel_id=1, source_target_pairs={{0,7},{1,0},{2,1},{3,2},{4,3},{5,4},{6,5},{7,6},{8,15},{9,8},{10,9... | collective-permute-start | bytes 1572872 | tf_op jit(solution)/shard_map/ppermute | solution.py:101
  43.3 4.5 %collective-permute-done.11 = f16[512,512]{1,0:T(8,128)(2,1)S(1)} collective-permute-done((f16[512,512]{1,0:T(8,128)(2,1)S(1)}, f16[512,512]{1,0:T(8,128)(2,1)S(1)}, u32[]{:S(2)}, u32[]{:S(2)}) %collective-permute-start.11) | collective-permute-done | bytes 524320 | tf_op jit(solution)/shard_map/ppermute | solution.py:156
  49.5 2.8 %collective-permute-start.14 = (f32[2,32,512]{2,1,0:T(8,128)S(1)}, f32[2,32,512]{2,1,0:T(8,128)S(1)}, u32[]{:S(2)}, u32[]{:S(2)}) collective-permute-start(f32[2,32,512]{2,1,0:T(8,128)S(1)} %dynamic-slice_bitcast_fusion.2), channel_id=1, source_target_pairs={{0,64},{16,80},{32,96},{48,112},{64,0},{80,16},{96,32},{112,48},{1... | collective-permute-start | bytes 393224 | tf_op jit(solution)/shard_map/ppermute | solution.py:85
  53.4 1.6 %collective-permute-done.14 = f32[2,32,512]{2,1,0:T(8,128)S(1)} collective-permute-done((f32[2,32,512]{2,1,0:T(8,128)S(1)}, f32[2,32,512]{2,1,0:T(8,128)S(1)}, u32[]{:S(2)}, u32[]{:S(2)}) %collective-permute-start.14) | collective-permute-done | bytes 131104 | tf_op jit(solution)/shard_map/ppermute | solution.py:85
  55.0 3.5 %collective-permute-done.13 = bf16[512,512]{1,0:T(8,128)(2,1)S(1)} collective-permute-done((bf16[512,512]{1,0:T(8,128)(2,1)S(1)}, bf16[512,512]{1,0:T(8,128)(2,1)S(1)}, u32[]{:S(2)}, u32[]{:S(2)}) %collective-permute-start.13) | collective-permute-done | bytes 524320 | tf_op jit(solution)/shard_map/ppermute | solution.py:101
  58.4 3.5 %collective-permute-start.20 = (f16[512,512]{1,0:T(8,128)(2,1)S(1)}, f16[512,512]{1,0:T(8,128)(2,1)S(1)}, u32[]{:S(2)}, u32[]{:S(2)}) collective-permute-start(f16[512,512]{1,0:T(8,128)(2,1)S(1)} %fusion.15), channel_id=1, source_target_pairs={{0,7},{1,0},{2,1},{3,2},{4,3},{5,4},{6,5},{7,6},{8,15},{9,8},{10,9... | collective-permute-start | bytes 1572872 | tf_op jit(solution)/shard_map/ppermute | solution.py:156
  64.0 2.5 %collective-permute-start.18 = (f32[32,512]{1,0:T(8,128)S(1)}, f32[32,512]{1,0:T(8,128)S(1)}, u32[]{:S(2)}, u32[]{:S(2)}) collective-permute-start(f32[32,512]{1,0:T(8,128)S(1)} %dynamic-slice_bitcast_fusion.3), channel_id=1, source_target_pairs={{0,128},{16,144},{32,160},{48,176},{64,192},{80,208},{96,224},{112... | collective-permute-start | bytes 196616 | tf_op jit(solution)/shard_map/ppermute | solution.py:85
  68.2 3.0 %collective-permute-start.22 = (bf16[512,512]{1,0:T(8,128)(2,1)S(1)}, bf16[512,512]{1,0:T(8,128)(2,1)S(1)}, u32[]{:S(2)}, u32[]{:S(2)}) collective-permute-start(bf16[512,512]{1,0:T(8,128)(2,1)S(1)} %collective-permute-done.13), channel_id=1, source_target_pairs={{0,7},{1,0},{2,1},{3,2},{4,3},{5,4},{6,5},{7,6},{8,15},{9,8},{10,9... | collective-permute-start | bytes 1572872 | tf_op jit(solution)/shard_map/ppermute | solution.py:101
  71.9 4.4 %collective-permute-done.18 = f32[32,512]{1,0:T(8,128)S(1)} collective-permute-done((f32[32,512]{1,0:T(8,128)S(1)}, f32[32,512]{1,0:T(8,128)S(1)}, u32[]{:S(2)}, u32[]{:S(2)}) %collective-permute-start.18) | collective-permute-done | bytes 65568 | tf_op jit(solution)/shard_map/ppermute | solution.py:85
  77.5 1.4 %collective-permute-start.26 = (f32[32,512]{1,0:T(8,128)S(1)}, f32[32,512]{1,0:T(8,128)S(1)}, u32[]{:S(2)}, u32[]{:S(2)}) collective-permute-start(f32[32,512]{1,0:T(8,128)S(1)} %get-tuple-element.178), channel_id=1, source_target_pairs={{0,128},{16,144},{32,160},{48,176},{64,192},{80,208},{96,224},{112... | collective-permute-start | bytes 196616 | tf_op jit(solution)/shard_map/ppermute | solution.py:91
  79.6 3.6 %collective-permute-start.31 = (f16[512,512]{1,0:T(8,128)(2,1)S(1)}, f16[512,512]{1,0:T(8,128)(2,1)S(1)}, u32[]{:S(2)}, u32[]{:S(2)}) collective-permute-start(f16[512,512]{1,0:T(8,128)(2,1)S(1)} %fusion.21), channel_id=1, source_target_pairs={{0,7},{1,0},{2,1},{3,2},{4,3},{5,4},{6,5},{7,6},{8,15},{9,8},{10,9... | collective-permute-start | bytes 1572872 | tf_op jit(solution)/shard_map/ppermute | solution.py:156
  84.9 1.4 %fusion.1 = f32[384,512]{1,0:T(8,128)S(1)} fusion(f32[384,512]{1,0:T(8,128)S(1)} %fusion.44, f32[384,512]{1,0:T(8,128)S(1)} %fusion, bf16[384,512]{1,0:T(8,128)(2,1)} %collective-permute-done.5, bf16[512,512]{1,0:T(8,128)(2,1)S(1)} %collective-permute-done.22), kind=kOutput, calls=%fused_computation.25 | convolution fusion | flops 201719808 | bytes 3276800 | tf_op jit(solution)/shard_map/dot_general | solution.py:176
  88.2 2.8 %collective-permute-start.27 = (f32[2,32,512]{2,1,0:T(8,128)S(1)}, f32[2,32,512]{2,1,0:T(8,128)S(1)}, u32[]{:S(2)}, u32[]{:S(2)}) collective-permute-start(f32[2,32,512]{2,1,0:T(8,128)S(1)} %pad_maximum_fusion.3), channel_id=1, source_target_pairs={{0,64},{16,80},{32,96},{48,112},{64,0},{80,16},{96,32},{112,48},{1... | collective-permute-start | bytes 393224 | tf_op jit(solution)/shard_map/ppermute | solution.py:91
  93.7 1.5 %fusion.7 = f32[384,512]{1,0:T(8,128)} fusion(f32[384,512]{1,0:T(8,128)S(1)} %fusion.51, f32[384,512]{1,0:T(8,128)S(1)} %fusion.50, f32[384,512]{1,0:T(8,128)S(1)} %fusion.49, f32[384,512]{1,0:T(8,128)S(1)} %fusion.48, f32[384,512]{1,0:T(8,128)S(1)} %fusion.47, f32[384,512]{1,0:T(8,128)S(1)} %fusion.46, f32[384,512]{1,0:T(8,128)S(1)} %fusion.45, ...), kind=kOutput, calls=%fused_computation.31 | convolution fusion | flops 202702848 | bytes 7208960 | tf_op jit(solution)/shard_map/dot_general | solution.py:176
  96.1 6.3 %collective-permute-done.28 = f32[2,2,32,512]{3,2,1,0:T(8,128)S(1)} collective-permute-done((f32[2,2,32,512]{3,2,1,0:T(8,128)S(1)}, f32[2,2,32,512]{3,2,1,0:T(8,128)S(1)}, u32[]{:S(2)}, u32[]{:S(2)}) %collective-permute-start.28) | collective-permute-done | bytes 262176 | tf_op jit(solution)/shard_map/ppermute | solution.py:91
  102.4 6.5 %collective-permute-start.29 = (f32[2,2,2,32,512]{4,3,2,1,0:T(8,128)S(1)}, f32[2,2,2,32,512]{4,3,2,1,0:T(8,128)S(1)}, u32[]{:S(2)}, u32[]{:S(2)}) collective-permute-start(f32[2,2,2,32,512]{4,3,2,1,0:T(8,128)S(1)} %pad_maximum_fusion.1), channel_id=1, source_target_pairs={{0,16},{16,0},{32,48},{48,32},{64,80},{80,64},{96,112},{112,96},{1... | collective-permute-start | bytes 1572872 | tf_op jit(solution)/shard_map/ppermute | solution.py:91
  109.4 1.4 %fusion.27 = f32[512,512]{1,0:T(8,128)} fusion(f16[512,512]{1,0:T(8,128)(2,1)S(1)} %collective-permute-done.31, f16[512,512]{1,0:T(8,128)(2,1)S(1)} %collective-permute-done.30, f32[512,512]{1,0:T(8,128)S(1)} %fusion.52, f32[512,512]{1,0:T(8,128)S(1)} %fusion.53), kind=kLoop, calls=%fused_computation.51 | loop fusion | flops 2883584 | bytes 4194304 | tf_op jit(solution)/shard_map/add | solution.py:148
  112.3 2.2 %add_convert_fusion = bf16[384,512]{1,0:T(8,128)(2,1)} fusion(f32[384,512]{1,0:T(8,128)} %fusion.7, f32[384,512]{1,0:T(8,128)} %collective-permute-done.25), kind=kLoop, calls=%fused_computation.54 | loop fusion | flops 393216 | bytes 1966080 | tf_op jit(solution)/shard_map/convert_element_type | solution.py:238
  (119 shorter events, 28.6 us)
Async XLA Ops:
  0.7 18.9 %collective-permute-start = (bf16[384,512]{1,0:T(8,128)(2,1)}, bf16[384,512]{1,0:T(8,128)(2,1)S(1)}, u32[]{:S(2)}, u32[]{:S(2)}) collective-permute-start(bf16[384,512]{1,0:T(8,128)(2,1)} %bitcast.138), channel_id=1, source_target_pairs={{0,8},{1,9},{2,10},{3,11},{4,12},{5,13},{6,14},{7,15},{8,0},{9,1},... | collective-permute-start | bytes 1179656 | tf_op jit(solution)/shard_map/ppermute | solution.py:77
  6.5 16.9 %collective-permute-start.2 = (bf16[512,512]{1,0:T(8,128)(2,1)S(1)}, bf16[512,512]{1,0:T(8,128)(2,1)S(1)}, u32[]{:S(2)}, u32[]{:S(2)}) collective-permute-start(bf16[512,512]{1,0:T(8,128)(2,1)S(1)} %bitcast.150), channel_id=1, source_target_pairs={{0,1},{1,2},{2,3},{3,4},{4,5},{5,6},{6,7},{7,0},{8,9},{9,10},{10,1... | collective-permute-start | bytes 1572872 | tf_op jit(solution)/shard_map/ppermute | solution.py:101
  8.2 15.3 %collective-permute-start.1 = (bf16[512,512]{1,0:T(8,128)(2,1)S(1)}, bf16[512,512]{1,0:T(8,128)(2,1)S(1)}, u32[]{:S(2)}, u32[]{:S(2)}) collective-permute-start(bf16[512,512]{1,0:T(8,128)(2,1)S(1)} %bitcast.151), channel_id=1, source_target_pairs={{0,7},{1,0},{2,1},{3,2},{4,3},{5,4},{6,5},{7,6},{8,15},{9,8},{10,9... | collective-permute-start | bytes 1572872 | tf_op jit(solution)/shard_map/ppermute | solution.py:101
  12.2 14.4 %collective-permute-start.5 = (bf16[384,512]{1,0:T(8,128)(2,1)}, bf16[384,512]{1,0:T(8,128)(2,1)}, u32[]{:S(2)}, u32[]{:S(2)}) collective-permute-start(bf16[384,512]{1,0:T(8,128)(2,1)} %get-tuple-element.226), channel_id=1, source_target_pairs={{0,8},{1,9},{2,10},{3,11},{4,12},{5,13},{6,14},{7,15},{8,0},{9,1},... | collective-permute-start | bytes 1179656 | tf_op jit(solution)/shard_map/ppermute | solution.py:77
  16.2 12.5 %collective-permute-start.4 = (bf16[2,2,2,32,512]{4,3,2,1,0:T(8,128)(2,1)}, bf16[2,2,2,32,512]{4,3,2,1,0:T(8,128)(2,1)}, u32[]{:S(2)}, u32[]{:S(2)}) collective-permute-start(bf16[2,2,2,32,512]{4,3,2,1,0:T(8,128)(2,1)} %dynamic-slice_bitcast_fusion.1), channel_id=1, source_target_pairs={{0,16},{16,0},{32,48},{48,32},{64,80},{80,64},{96,112},{112,96},{1... | collective-permute-start | bytes 786440 | tf_op jit(solution)/shard_map/ppermute | solution.py:85
  21.7 10.8 %collective-permute-start.9 = (bf16[384,512]{1,0:T(8,128)(2,1)S(1)}, bf16[384,512]{1,0:T(8,128)(2,1)S(1)}, u32[]{:S(2)}, u32[]{:S(2)}) collective-permute-start(bf16[384,512]{1,0:T(8,128)(2,1)S(1)} %copy-done.11), channel_id=1, source_target_pairs={{0,8},{1,9},{2,10},{3,11},{4,12},{5,13},{6,14},{7,15},{8,0},{9,1},... | collective-permute-start | bytes 1179656 | tf_op jit(solution)/shard_map/ppermute | solution.py:77
  23.4 13.1 %collective-permute-start.8 = (bf16[512,512]{1,0:T(8,128)(2,1)S(1)}, bf16[512,512]{1,0:T(8,128)(2,1)S(1)}, u32[]{:S(2)}, u32[]{:S(2)}) collective-permute-start(bf16[512,512]{1,0:T(8,128)(2,1)S(1)} %collective-permute-done.2), channel_id=1, source_target_pairs={{0,1},{1,2},{2,3},{3,4},{4,5},{5,6},{6,7},{7,0},{8,9},{9,10},{10,1... | collective-permute-start | bytes 1572872 | tf_op jit(solution)/shard_map/ppermute | solution.py:101
  23.4 13.5 %collective-permute-start.7 = (bf16[512,512]{1,0:T(8,128)(2,1)S(1)}, bf16[512,512]{1,0:T(8,128)(2,1)S(1)}, u32[]{:S(2)}, u32[]{:S(2)}) collective-permute-start(bf16[512,512]{1,0:T(8,128)(2,1)S(1)} %collective-permute-done.1), channel_id=1, source_target_pairs={{0,7},{1,0},{2,1},{3,2},{4,3},{5,4},{6,5},{7,6},{8,15},{9,8},{10,9... | collective-permute-start | bytes 1572872 | tf_op jit(solution)/shard_map/ppermute | solution.py:101
  30.6 9.9 %collective-permute-start.3 = (bf16[384,512]{1,0:T(8,128)(2,1)S(1)}, bf16[384,512]{1,0:T(8,128)(2,1)S(1)}, u32[]{:S(2)}, u32[]{:S(2)}) collective-permute-start(bf16[384,512]{1,0:T(8,128)(2,1)S(1)} %copy-done.10), channel_id=1, source_target_pairs={{0,8},{1,9},{2,10},{3,11},{4,12},{5,13},{6,14},{7,15},{8,0},{9,1},... | collective-permute-start | bytes 1179656 | tf_op jit(solution)/shard_map/ppermute | solution.py:77
  31.1 16.7 %collective-permute-start.11 = (f16[512,512]{1,0:T(8,128)(2,1)S(1)}, f16[512,512]{1,0:T(8,128)(2,1)S(1)}, u32[]{:S(2)}, u32[]{:S(2)}) collective-permute-start(f16[512,512]{1,0:T(8,128)(2,1)S(1)} %fusion.8), channel_id=1, source_target_pairs={{0,1},{1,2},{2,3},{3,4},{4,5},{5,6},{6,7},{7,0},{8,9},{9,10},{10,1... | collective-permute-start | bytes 1572872 | tf_op jit(solution)/shard_map/ppermute | solution.py:156
  32.5 6.8 %collective-permute-start.6 = (f32[2,2,32,512]{3,2,1,0:T(8,128)S(1)}, f32[2,2,32,512]{3,2,1,0:T(8,128)S(1)}, u32[]{:S(2)}, u32[]{:S(2)}) collective-permute-start(f32[2,2,32,512]{3,2,1,0:T(8,128)S(1)} %dynamic-slice_bitcast_fusion), channel_id=1, source_target_pairs={{0,32},{16,48},{32,0},{48,16},{64,96},{80,112},{96,64},{112,80},{1... | collective-permute-start | bytes 786440 | tf_op jit(solution)/shard_map/ppermute | solution.py:85
  36.5 12.4 %collective-permute-start.10 = (bf16[384,512]{1,0:T(8,128)(2,1)S(1)}, bf16[384,512]{1,0:T(8,128)(2,1)S(1)}, u32[]{:S(2)}, u32[]{:S(2)}) collective-permute-start(bf16[384,512]{1,0:T(8,128)(2,1)S(1)} %copy-done.9), channel_id=1, source_target_pairs={{0,8},{1,9},{2,10},{3,11},{4,12},{5,13},{6,14},{7,15},{8,0},{9,1},... | collective-permute-start | bytes 1179656 | tf_op jit(solution)/shard_map/ppermute | solution.py:77
  37.0 12.6 %collective-permute-start.15 = (f16[512,512]{1,0:T(8,128)(2,1)S(1)}, f16[512,512]{1,0:T(8,128)(2,1)S(1)}, u32[]{:S(2)}, u32[]{:S(2)}) collective-permute-start(f16[512,512]{1,0:T(8,128)(2,1)S(1)} %fusion.9), channel_id=1, source_target_pairs={{0,7},{1,0},{2,1},{3,2},{4,3},{5,4},{6,5},{7,6},{8,15},{9,8},{10,9... | collective-permute-start | bytes 1572872 | tf_op jit(solution)/shard_map/ppermute | solution.py:156
  39.4 19.1 %collective-permute-start.12 = (bf16[384,512]{1,0:T(8,128)(2,1)S(1)}, bf16[384,512]{1,0:T(8,128)(2,1)S(1)}, u32[]{:S(2)}, u32[]{:S(2)}) collective-permute-start(bf16[384,512]{1,0:T(8,128)(2,1)S(1)} %copy-done.8), channel_id=1, source_target_pairs={{0,8},{1,9},{2,10},{3,11},{4,12},{5,13},{6,14},{7,15},{8,0},{9,1},... | collective-permute-start | bytes 1179656 | tf_op jit(solution)/shard_map/ppermute | solution.py:77
  40.5 17.9 %collective-permute-start.13 = (bf16[512,512]{1,0:T(8,128)(2,1)S(1)}, bf16[512,512]{1,0:T(8,128)(2,1)S(1)}, u32[]{:S(2)}, u32[]{:S(2)}) collective-permute-start(bf16[512,512]{1,0:T(8,128)(2,1)S(1)} %collective-permute-done.7), channel_id=1, source_target_pairs={{0,7},{1,0},{2,1},{3,2},{4,3},{5,4},{6,5},{7,6},{8,15},{9,8},{10,9... | collective-permute-start | bytes 1572872 | tf_op jit(solution)/shard_map/ppermute | solution.py:101
  48.4 15.6 %collective-permute-start.19 = (f16[512,512]{1,0:T(8,128)(2,1)S(1)}, f16[512,512]{1,0:T(8,128)(2,1)S(1)}, u32[]{:S(2)}, u32[]{:S(2)}) collective-permute-start(f16[512,512]{1,0:T(8,128)(2,1)S(1)} %fusion.12), channel_id=1, source_target_pairs={{0,1},{1,2},{2,3},{3,4},{4,5},{5,6},{6,7},{7,0},{8,9},{9,10},{10,1... | collective-permute-start | bytes 1572872 | tf_op jit(solution)/shard_map/ppermute | solution.py:156
  49.0 18.7 %collective-permute-start.16 = (bf16[384,512]{1,0:T(8,128)(2,1)S(1)}, bf16[384,512]{1,0:T(8,128)(2,1)S(1)}, u32[]{:S(2)}, u32[]{:S(2)}) collective-permute-start(bf16[384,512]{1,0:T(8,128)(2,1)S(1)} %copy-done.7), channel_id=1, source_target_pairs={{0,8},{1,9},{2,10},{3,11},{4,12},{5,13},{6,14},{7,15},{8,0},{9,1},... | collective-permute-start | bytes 1179656 | tf_op jit(solution)/shard_map/ppermute | solution.py:77
  49.5 5.4 %collective-permute-start.14 = (f32[2,32,512]{2,1,0:T(8,128)S(1)}, f32[2,32,512]{2,1,0:T(8,128)S(1)}, u32[]{:S(2)}, u32[]{:S(2)}) collective-permute-start(f32[2,32,512]{2,1,0:T(8,128)S(1)} %dynamic-slice_bitcast_fusion.2), channel_id=1, source_target_pairs={{0,64},{16,80},{32,96},{48,112},{64,0},{80,16},{96,32},{112,48},{1... | collective-permute-start | bytes 393224 | tf_op jit(solution)/shard_map/ppermute | solution.py:85
  54.9 22.6 %collective-permute-start.17 = (bf16[512,512]{1,0:T(8,128)(2,1)S(1)}, bf16[512,512]{1,0:T(8,128)(2,1)S(1)}, u32[]{:S(2)}, u32[]{:S(2)}) collective-permute-start(bf16[512,512]{1,0:T(8,128)(2,1)S(1)} %collective-permute-done.8), channel_id=1, source_target_pairs={{0,1},{1,2},{2,3},{3,4},{4,5},{5,6},{6,7},{7,0},{8,9},{9,10},{10,1... | collective-permute-start | bytes 1572872 | tf_op jit(solution)/shard_map/ppermute | solution.py:101
  58.4 21.2 %collective-permute-start.21 = (bf16[384,512]{1,0:T(8,128)(2,1)S(1)}, bf16[384,512]{1,0:T(8,128)(2,1)S(1)}, u32[]{:S(2)}, u32[]{:S(2)}) collective-permute-start(bf16[384,512]{1,0:T(8,128)(2,1)S(1)} %copy-done.6), channel_id=1, source_target_pairs={{0,8},{1,9},{2,10},{3,11},{4,12},{5,13},{6,14},{7,15},{8,0},{9,1},... | collective-permute-start | bytes 1179656 | tf_op jit(solution)/shard_map/ppermute | solution.py:77
  58.4 9.8 %collective-permute-start.20 = (f16[512,512]{1,0:T(8,128)(2,1)S(1)}, f16[512,512]{1,0:T(8,128)(2,1)S(1)}, u32[]{:S(2)}, u32[]{:S(2)}) collective-permute-start(f16[512,512]{1,0:T(8,128)(2,1)S(1)} %fusion.15), channel_id=1, source_target_pairs={{0,7},{1,0},{2,1},{3,2},{4,3},{5,4},{6,5},{7,6},{8,15},{9,8},{10,9... | collective-permute-start | bytes 1572872 | tf_op jit(solution)/shard_map/ppermute | solution.py:156
  64.0 12.2 %collective-permute-start.18 = (f32[32,512]{1,0:T(8,128)S(1)}, f32[32,512]{1,0:T(8,128)S(1)}, u32[]{:S(2)}, u32[]{:S(2)}) collective-permute-start(f32[32,512]{1,0:T(8,128)S(1)} %dynamic-slice_bitcast_fusion.3), channel_id=1, source_target_pairs={{0,128},{16,144},{32,160},{48,176},{64,192},{80,208},{96,224},{112... | collective-permute-start | bytes 196616 | tf_op jit(solution)/shard_map/ppermute | solution.py:85
  67.7 16.1 %collective-permute-start.23 = (f16[512,512]{1,0:T(8,128)(2,1)S(1)}, f16[512,512]{1,0:T(8,128)(2,1)S(1)}, u32[]{:S(2)}, u32[]{:S(2)}) collective-permute-start(f16[512,512]{1,0:T(8,128)(2,1)S(1)} %fusion.18), channel_id=1, source_target_pairs={{0,1},{1,2},{2,3},{3,4},{4,5},{5,6},{6,7},{7,0},{8,9},{9,10},{10,1... | collective-permute-start | bytes 1572872 | tf_op jit(solution)/shard_map/ppermute | solution.py:156
  68.2 16.3 %collective-permute-start.22 = (bf16[512,512]{1,0:T(8,128)(2,1)S(1)}, bf16[512,512]{1,0:T(8,128)(2,1)S(1)}, u32[]{:S(2)}, u32[]{:S(2)}) collective-permute-start(bf16[512,512]{1,0:T(8,128)(2,1)S(1)} %collective-permute-done.13), channel_id=1, source_target_pairs={{0,7},{1,0},{2,1},{3,2},{4,3},{5,4},{6,5},{7,6},{8,15},{9,8},{10,9... | collective-permute-start | bytes 1572872 | tf_op jit(solution)/shard_map/ppermute | solution.py:101
  76.3 10.0 %collective-permute-start.24 = (bf16[384,512]{1,0:T(8,128)(2,1)S(1)}, bf16[384,512]{1,0:T(8,128)(2,1)S(1)}, u32[]{:S(2)}, u32[]{:S(2)}) collective-permute-start(bf16[384,512]{1,0:T(8,128)(2,1)S(1)} %copy-done.5), channel_id=1, source_target_pairs={{0,8},{1,9},{2,10},{3,11},{4,12},{5,13},{6,14},{7,15},{8,0},{9,1},... | collective-permute-start | bytes 1179656 | tf_op jit(solution)/shard_map/ppermute | solution.py:77
  77.5 10.7 %collective-permute-start.26 = (f32[32,512]{1,0:T(8,128)S(1)}, f32[32,512]{1,0:T(8,128)S(1)}, u32[]{:S(2)}, u32[]{:S(2)}) collective-permute-start(f32[32,512]{1,0:T(8,128)S(1)} %get-tuple-element.178), channel_id=1, source_target_pairs={{0,128},{16,144},{32,160},{48,176},{64,192},{80,208},{96,224},{112... | collective-permute-start | bytes 196616 | tf_op jit(solution)/shard_map/ppermute | solution.py:91
  79.6 29.7 %collective-permute-start.31 = (f16[512,512]{1,0:T(8,128)(2,1)S(1)}, f16[512,512]{1,0:T(8,128)(2,1)S(1)}, u32[]{:S(2)}, u32[]{:S(2)}) collective-permute-start(f16[512,512]{1,0:T(8,128)(2,1)S(1)} %fusion.21), channel_id=1, source_target_pairs={{0,7},{1,0},{2,1},{3,2},{4,3},{5,4},{6,5},{7,6},{8,15},{9,8},{10,9... | collective-permute-start | bytes 1572872 | tf_op jit(solution)/shard_map/ppermute | solution.py:156
  84.4 24.9 %collective-permute-start.30 = (f16[512,512]{1,0:T(8,128)(2,1)S(1)}, f16[512,512]{1,0:T(8,128)(2,1)S(1)}, u32[]{:S(2)}, u32[]{:S(2)}) collective-permute-start(f16[512,512]{1,0:T(8,128)(2,1)S(1)} %fusion.24), channel_id=1, source_target_pairs={{0,1},{1,2},{2,3},{3,4},{4,5},{5,6},{6,7},{7,0},{8,9},{9,10},{10,1... | collective-permute-start | bytes 1572872 | tf_op jit(solution)/shard_map/ppermute | solution.py:156
  87.6 24.7 %collective-permute-start.25 = (f32[384,512]{1,0:T(8,128)}, f32[384,512]{1,0:T(8,128)}, u32[]{:S(2)}, u32[]{:S(2)}) collective-permute-start(f32[384,512]{1,0:T(8,128)} %convolution_add_fusion.5), channel_id=1, source_target_pairs={{0,8},{1,9},{2,10},{3,11},{4,12},{5,13},{6,14},{7,15},{8,0},{9,1},... | collective-permute-start | bytes 2359304 | tf_op jit(solution)/shard_map/ppermute | solution.py:77
  88.2 6.9 %collective-permute-start.27 = (f32[2,32,512]{2,1,0:T(8,128)S(1)}, f32[2,32,512]{2,1,0:T(8,128)S(1)}, u32[]{:S(2)}, u32[]{:S(2)}) collective-permute-start(f32[2,32,512]{2,1,0:T(8,128)S(1)} %pad_maximum_fusion.3), channel_id=1, source_target_pairs={{0,64},{16,80},{32,96},{48,112},{64,0},{80,16},{96,32},{112,48},{1... | collective-permute-start | bytes 393224 | tf_op jit(solution)/shard_map/ppermute | solution.py:91
  95.2 7.1 %collective-permute-start.28 = (f32[2,2,32,512]{3,2,1,0:T(8,128)S(1)}, f32[2,2,32,512]{3,2,1,0:T(8,128)S(1)}, u32[]{:S(2)}, u32[]{:S(2)}) collective-permute-start(f32[2,2,32,512]{3,2,1,0:T(8,128)S(1)} %pad_maximum_fusion.2), channel_id=1, source_target_pairs={{0,32},{16,48},{32,0},{48,16},{64,96},{80,112},{96,64},{112,80},{1... | collective-permute-start | bytes 786440 | tf_op jit(solution)/shard_map/ppermute | solution.py:91
  102.4 8.3 %collective-permute-start.29 = (f32[2,2,2,32,512]{4,3,2,1,0:T(8,128)S(1)}, f32[2,2,2,32,512]{4,3,2,1,0:T(8,128)S(1)}, u32[]{:S(2)}, u32[]{:S(2)}) collective-permute-start(f32[2,2,2,32,512]{4,3,2,1,0:T(8,128)S(1)} %pad_maximum_fusion.1), channel_id=1, source_target_pairs={{0,16},{16,0},{32,48},{48,32},{64,80},{80,64},{96,112},{112,96},{1... | collective-permute-start | bytes 1572872 | tf_op jit(solution)/shard_map/ppermute | solution.py:91
  (13 other events, 163.0 us)

commit v3 on v2

--- a/solution.py
+++ b/solution.py
@@ -126,9 +126,28 @@
         nonlocal part, sent
         sent, part = order.gate(sent, part)
         part = fold(part, sent, b)
-        if b < 3:
+        if b < 2:
             sent = fold_send(part, b + 1)
+        else:
+            part = jnp.concatenate([part.reshape(2 * cols, rows), outer_momentum.T], 0)
+            sent = spread_send(part, 3)
         order.done(part)
+
+    def outer_step():
+        nonlocal part, sent
+        sent, part = order.gate(sent, part)
+        total = part[: 2 * cols] + sent[: 2 * cols]
+        low = bits[3] == 0
+        momentum = jnp.concatenate(
+            [jnp.where(low, part[2 * cols :], sent[2 * cols :]), jnp.where(low, sent[2 * cols :], part[2 * cols :])], 0
+        )
+        both = global_fragment.T.reshape(2, 8, cols, rows)
+        mine = pick(both, island & 7, 1).reshape(2 * cols, rows)
+        pseudo = mine - total / 16
+        momentum = outer_mu * momentum + pseudo
+        new = mine - outer_rate * (pseudo + outer_mu * momentum)
+        order.done(new)
+        return new.reshape(2, cols, rows), pick(momentum.reshape(2, cols, rows), bits[3], 0)
 
     def spread_step(b):
         nonlocal full, sent
@@ -212,20 +231,14 @@
     ring(4)
     own_dots(5)
     ring(5)
-    fold_step(3)
-    mine = lax.dynamic_slice_in_dim(global_fragment.T, island * cols, cols, 0)
-    pseudo = mine - part / 16
-    momentum = outer_mu * outer_momentum.T + pseudo
-    full = mine - outer_rate * (pseudo + outer_mu * momentum)
-    sent = spread_send(full, 3)
-    order.done(full)
     own_dots(6)
     partner = theirs((1, 5), partner)
     ring(6)
     partner = theirs((0, 6), partner)
     partner = theirs((7,), partner)
     back = over_y(partner)
-    spread_step(3)
+    full, momentum = outer_step()
+    sent = spread_send(full, 2)
     forward = products(ours, range(Z), None)
     spread_step(2)
     own_dots(7)

time: 115 us -> 113 us (0.983)
  matrix products: 18.2 us -> 14.5 us
  waiting for transfers between devices: 24.4 us -> 26.3 us
  starting transfers between devices: 49.1 us -> 50.7 us
    ppermute x7, waiting for transfers between devices: 4.5 us -> 10.2 us  [ring(): carry[way] = lax.ppermute(g, 'fsdp', UP if way > 0 else DOWN)]
    ppermute x4 -> x3, waiting for transfers between devices: 6.41 us -> 1.59 us  [fold_send(): return lax.ppermute(pick(part, 1 - bits[b], 3 - b), 'island', xor(1 << b))]
    ppermute x4, starting transfers between devices: 11 us -> 15.8 us  [spread_send(): return lax.ppermute(full, 'island', xor(1 << b))]
    ppermute x7, starting transfers between devices: 9.33 us -> 6.53 us  [ring(): carry[way] = lax.ppermute(g, 'fsdp', UP if way > 0 else DOWN)]
    dot_general x16, matrix products: 8.86 us -> 6.12 us  [products(): d = jnp.dot(got, rows_w, preferred_element_type=f32)]
    ppermute x4 -> x3, starting transfers between devices: 7.97 us -> 5.64 us  [fold_send(): return lax.ppermute(pick(part, 1 - bits[b], 3 - b), 'island', xor(1 << b))]
    ppermute x7, waiting for transfers between devices: 5.76 us -> 7.81 us  [w_hop(): lax.ppermute(w[-way * (h - 1)], 'fsdp', UP if way > 0 else DOWN)]
    squeeze x4 -> x3, local copies, waits for them, and re-layouts: 1.73 us -> 0.05 us  [pick(): return lax.dynamic_index_in_dim(a, i, axis, keepdims=False)]
  transfers between devices with their start and end apart: 32 -> 31, of which waited for: 9 -> 8; matrix products, arithmetic and copies ran while one was open for 33% -> 29% of each run, Pallas kernels for 0% -> 0%
where the time goes in v3:
time: 113 us
  starting transfers between devices  50.7 us (45%)
  waiting for transfers between devices  26.3 us (23%)
  matrix products  14.5 us (13%)
  local copies, waits for them, and re-layouts  12.5 us (11%)
  other arithmetic  8.03 us (7%)
  between operations  1.22 us (1%)
    ppermute x4, starting transfers between devices, spread_send(): return lax.ppermute(full, 'island', xor(1 << b))  15.8 us
    ppermute x7, starting transfers between devices, w_hop(): lax.ppermute(w[-way * (h - 1)], 'fsdp', UP if way > 0 else DOWN)  14.6 us
    ppermute x7, waiting for transfers between devices, ring(): carry[way] = lax.ppermute(g, 'fsdp', UP if way > 0 else DOWN)  10.2 us
    dot_general x16, matrix products, tn(): lax.dot_general(a, b, (((0,), (0,)), ((), ())), preferred_element_type=f32)  8.34 us
    ppermute x10, starting transfers between devices, over_y(): return lax.ppermute(x, 'fsdp', PAIR)  8.11 us
    ppermute x7, waiting for transfers between devices, w_hop(): lax.ppermute(w[-way * (h - 1)], 'fsdp', UP if way > 0 else DOWN)  7.81 us
    ppermute x7, starting transfers between devices, ring(): carry[way] = lax.ppermute(g, 'fsdp', UP if way > 0 else DOWN)  6.53 us
    dot_general x16, matrix products, products(): d = jnp.dot(got, rows_w, preferred_element_type=f32)  6.12 us
  transfers between devices with their start and end apart: 31, of which 8 were waited for; matrix products, arithmetic and copies ran while one was open for 29% of the time, Pallas kernels for 0%

profile of v3, /device:TPU:1, one launch (start us, length us, event | category | flops | bytes accessed | tf_op | source)
XLA Modules:
  0.0 113.1 jit_solution(7251895591503960546)
XLA Ops:
  0.6 2.2 %collective-permute-start = (bf16[384,512]{1,0:T(8,128)(2,1)}, bf16[384,512]{1,0:T(8,128)(2,1)S(1)}, u32[]{:S(2)}, u32[]{:S(2)}) collective-permute-start(bf16[384,512]{1,0:T(8,128)(2,1)} %bitcast.120), channel_id=1, source_target_pairs={{0,8},{1,9},{2,10},{3,11},{4,12},{5,13},{6,14},{7,15},{8,0},{9,1},... | collective-permute-start | bytes 1179656 | tf_op jit(solution)/shard_map/ppermute | solution.py:77
  2.9 3.6 %constant_dynamic-slice_fusion.9 = (bf16[384,512]{1,0:T(8,128)(2,1)}, bf16[384,512]{1,0:T(8,128)(2,1)}, bf16[384,512]{1,0:T(8,128)(2,1)}, bf16[384,512]{1,0:T(8,...) fusion(bf16[384,8192]{1,0:T(8,128)(2,1)} %bitcast.129, ...), kind=kLoop, calls=%fused_computation.86 | loop fusion | bytes 6291488 | tf_op jit(solution)/shard_map/dynamic_slice | solution.py:71
  6.4 1.7 %collective-permute-start.2 = (bf16[512,512]{1,0:T(8,128)(2,1)S(1)}, bf16[512,512]{1,0:T(8,128)(2,1)S(1)}, u32[]{:S(2)}, u32[]{:S(2)}) collective-permute-start(bf16[512,512]{1,0:T(8,128)(2,1)S(1)} %bitcast.132), channel_id=1, source_target_pairs={{0,1},{1,2},{2,3},{3,4},{4,5},{5,6},{6,7},{7,0},{8,9},{9,10},{10,1... | collective-permute-start | bytes 1572872 | tf_op jit(solution)/shard_map/ppermute | solution.py:101
  8.1 4.0 %collective-permute-start.1 = (bf16[512,512]{1,0:T(8,128)(2,1)S(1)}, bf16[512,512]{1,0:T(8,128)(2,1)S(1)}, u32[]{:S(2)}, u32[]{:S(2)}) collective-permute-start(bf16[512,512]{1,0:T(8,128)(2,1)S(1)} %bitcast.133), channel_id=1, source_target_pairs={{0,7},{1,0},{2,1},{3,2},{4,3},{5,4},{6,5},{7,6},{8,15},{9,8},{10,9... | collective-permute-start | bytes 1572872 | tf_op jit(solution)/shard_map/ppermute | solution.py:101
  12.3 1.3 %copy.18 = bf16[1,512,512]{1,2,0:T(8,128)(2,1)S(1)} copy(bf16[1,512,512]{2,1,0:T(8,128)(2,1)} %param.9) | data formatting | bytes 1048576 | tf_op args[3]
  13.6 1.6 %collective-permute-start.4 = (bf16[2,2,2,32,512]{4,3,2,1,0:T(8,128)(2,1)S(1)}, bf16[2,2,2,32,512]{4,3,2,1,0:T(8,128)(2,1)}, u32[]{:S(2)}, u32[]{:S(2)}) collective-permute-start(bf16[2,2,2,32,512]{4,3,2,1,0:T(8,128)(2,1)S(1)} %dynamic-slice_bitcast_fusion.1), channel_id=1, source_target_pairs={{0,16},{16,0},{32,48},{48,32},{64,80},{80,64},{96,112},{112,96},{1... | collective-permute-start | bytes 786440 | tf_op jit(solution)/shard_map/ppermute | solution.py:85
  15.2 2.5 %copy.19 = f32[512,512]{0,1:T(8,128)} copy(f32[512,512]{1,0:T(8,128)} %param.10) | data formatting | bytes 2097152 | tf_op args[4]
  18.7 2.1 %constant_dynamic-slice_fusion.1 = (bf16[384,512]{1,0:T(8,128)(2,1)S(1)}, bf16[384,512]{1,0:T(8,128)(2,1)S(1)}, bf16[384,512]{1,0:T(8,128)(2,1)S(1)}, bf16[384,5...) fusion(bf16[384,8192]{1,0:T(8,128)(2,1)} %bitcast.130, ...), kind=kLoop, calls=%fused_computation.78 | loop fusion | bytes 6291488 | tf_op jit(solution)/shard_map/dynamic_slice | solution.py:71
  20.8 1.4 %collective-permute-start.9 = (bf16[384,512]{1,0:T(8,128)(2,1)S(1)}, bf16[384,512]{1,0:T(8,128)(2,1)S(1)}, u32[]{:S(2)}, u32[]{:S(2)}) collective-permute-start(bf16[384,512]{1,0:T(8,128)(2,1)S(1)} %copy-done.8), channel_id=1, source_target_pairs={{0,8},{1,9},{2,10},{3,11},{4,12},{5,13},{6,14},{7,15},{8,0},{9,1},... | collective-permute-start | bytes 1179656 | tf_op jit(solution)/shard_map/ppermute | solution.py:77
  22.2 1.2 %collective-permute-done.2 = bf16[512,512]{1,0:T(8,128)(2,1)S(1)} collective-permute-done((bf16[512,512]{1,0:T(8,128)(2,1)S(1)}, bf16[512,512]{1,0:T(8,128)(2,1)S(1)}, u32[]{:S(2)}, u32[]{:S(2)}) %collective-permute-start.2) | collective-permute-done | bytes 524320 | tf_op jit(solution)/shard_map/ppermute | solution.py:101
  23.4 2.7 %collective-permute-start.7 = (bf16[512,512]{1,0:T(8,128)(2,1)S(1)}, bf16[512,512]{1,0:T(8,128)(2,1)S(1)}, u32[]{:S(2)}, u32[]{:S(2)}) collective-permute-start(bf16[512,512]{1,0:T(8,128)(2,1)S(1)} %collective-permute-done.1), channel_id=1, source_target_pairs={{0,7},{1,0},{2,1},{3,2},{4,3},{5,4},{6,5},{7,6},{8,15},{9,8},{10,9... | collective-permute-start | bytes 1572872 | tf_op jit(solution)/shard_map/ppermute | solution.py:101
  27.6 1.0 convert_add_fusion
  29.8 1.8 %collective-permute-done.9 = bf16[384,512]{1,0:T(8,128)(2,1)S(1)} collective-permute-done((bf16[384,512]{1,0:T(8,128)(2,1)S(1)}, bf16[384,512]{1,0:T(8,128)(2,1)S(1)}, u32[]{:S(2)}, u32[]{:S(2)}) %collective-permute-start.9) | collective-permute-done | bytes 393248 | tf_op jit(solution)/shard_map/ppermute | solution.py:77
  31.6 1.2 %collective-permute-start.6 = (f32[2,2,32,512]{3,2,1,0:T(8,128)S(1)}, f32[2,2,32,512]{3,2,1,0:T(8,128)S(1)}, u32[]{:S(2)}, u32[]{:S(2)}) collective-permute-start(f32[2,2,32,512]{3,2,1,0:T(8,128)S(1)} %dynamic-slice_bitcast_fusion), channel_id=1, source_target_pairs={{0,32},{16,48},{32,0},{48,16},{64,96},{80,112},{96,64},{112,80},{1... | collective-permute-start | bytes 786440 | tf_op jit(solution)/shard_map/ppermute | solution.py:85
  33.7 2.8 %collective-permute-done.8 = bf16[512,512]{1,0:T(8,128)(2,1)S(1)} collective-permute-done((bf16[512,512]{1,0:T(8,128)(2,1)S(1)}, bf16[512,512]{1,0:T(8,128)(2,1)S(1)}, u32[]{:S(2)}, u32[]{:S(2)}) %collective-permute-start.8) | collective-permute-done | bytes 524320 | tf_op jit(solution)/shard_map/ppermute | solution.py:101
  36.7 2.2 %collective-permute-start.15 = (f16[512,512]{1,0:T(8,128)(2,1)S(1)}, f16[512,512]{1,0:T(8,128)(2,1)S(1)}, u32[]{:S(2)}, u32[]{:S(2)}) collective-permute-start(f16[512,512]{1,0:T(8,128)(2,1)S(1)} %fusion.9), channel_id=1, source_target_pairs={{0,7},{1,0},{2,1},{3,2},{4,3},{5,4},{6,5},{7,6},{8,15},{9,8},{10,9... | collective-permute-start | bytes 1572872 | tf_op jit(solution)/shard_map/ppermute | solution.py:175
  39.5 3.1 %collective-permute-start.13 = (bf16[512,512]{1,0:T(8,128)(2,1)S(1)}, bf16[512,512]{1,0:T(8,128)(2,1)S(1)}, u32[]{:S(2)}, u32[]{:S(2)}) collective-permute-start(bf16[512,512]{1,0:T(8,128)(2,1)S(1)} %collective-permute-done.7), channel_id=1, source_target_pairs={{0,7},{1,0},{2,1},{3,2},{4,3},{5,4},{6,5},{7,6},{8,15},{9,8},{10,9... | collective-permute-start | bytes 1572872 | tf_op jit(solution)/shard_map/ppermute | solution.py:101
  43.1 4.6 %collective-permute-done.11 = f16[512,512]{1,0:T(8,128)(2,1)S(1)} collective-permute-done((f16[512,512]{1,0:T(8,128)(2,1)S(1)}, f16[512,512]{1,0:T(8,128)(2,1)S(1)}, u32[]{:S(2)}, u32[]{:S(2)}) %collective-permute-start.11) | collective-permute-done | bytes 524320 | tf_op jit(solution)/shard_map/ppermute | solution.py:175
  49.2 2.8 %collective-permute-start.14 = (f32[2,32,512]{2,1,0:T(8,128)S(1)}, f32[2,32,512]{2,1,0:T(8,128)S(1)}, u32[]{:S(2)}, u32[]{:S(2)}) collective-permute-start(f32[2,32,512]{2,1,0:T(8,128)S(1)} %dynamic-slice_bitcast_fusion.2), channel_id=1, source_target_pairs={{0,64},{16,80},{32,96},{48,112},{64,0},{80,16},{96,32},{112,48},{1... | collective-permute-start | bytes 393224 | tf_op jit(solution)/shard_map/ppermute | solution.py:85
  53.0 1.6 %collective-permute-done.14 = f32[2,32,512]{2,1,0:T(8,128)S(1)} collective-permute-done((f32[2,32,512]{2,1,0:T(8,128)S(1)}, f32[2,32,512]{2,1,0:T(8,128)S(1)}, u32[]{:S(2)}, u32[]{:S(2)}) %collective-permute-start.14) | collective-permute-done | bytes 131104 | tf_op jit(solution)/shard_map/ppermute | solution.py:85
  54.7 3.8 %collective-permute-done.13 = bf16[512,512]{1,0:T(8,128)(2,1)S(1)} collective-permute-done((bf16[512,512]{1,0:T(8,128)(2,1)S(1)}, bf16[512,512]{1,0:T(8,128)(2,1)S(1)}, u32[]{:S(2)}, u32[]{:S(2)}) %collective-permute-start.13) | collective-permute-done | bytes 524320 | tf_op jit(solution)/shard_map/ppermute | solution.py:101
  58.5 3.5 %collective-permute-start.19 = (f16[512,512]{1,0:T(8,128)(2,1)S(1)}, f16[512,512]{1,0:T(8,128)(2,1)S(1)}, u32[]{:S(2)}, u32[]{:S(2)}) collective-permute-start(f16[512,512]{1,0:T(8,128)(2,1)S(1)} %fusion.15), channel_id=1, source_target_pairs={{0,7},{1,0},{2,1},{3,2},{4,3},{5,4},{6,5},{7,6},{8,15},{9,8},{10,9... | collective-permute-start | bytes 1572872 | tf_op jit(solution)/shard_map/ppermute | solution.py:175
  64.1 2.4 %collective-permute-start.25 = (f32[96,512]{1,0:T(8,128)S(1)}, f32[96,512]{1,0:T(8,128)S(1)}, u32[]{:S(2)}, u32[]{:S(2)}) collective-permute-start(f32[96,512]{1,0:T(8,128)S(1)} %pad_maximum_fusion.3), channel_id=1, source_target_pairs={{0,128},{16,144},{32,160},{48,176},{64,192},{80,208},{96,224},{112... | collective-permute-start | bytes 589832 | tf_op jit(solution)/shard_map/ppermute | solution.py:91
  68.2 3.1 %collective-permute-start.21 = (bf16[512,512]{1,0:T(8,128)(2,1)S(1)}, bf16[512,512]{1,0:T(8,128)(2,1)S(1)}, u32[]{:S(2)}, u32[]{:S(2)}) collective-permute-start(bf16[512,512]{1,0:T(8,128)(2,1)S(1)} %collective-permute-done.13), channel_id=1, source_target_pairs={{0,7},{1,0},{2,1},{3,2},{4,3},{5,4},{6,5},{7,6},{8,15},{9,8},{10,9... | collective-permute-start | bytes 1572872 | tf_op jit(solution)/shard_map/ppermute | solution.py:101
  72.4 2.6 %collective-permute-start.23 = (bf16[384,512]{1,0:T(8,128)(2,1)S(1)}, bf16[384,512]{1,0:T(8,128)(2,1)S(1)}, u32[]{:S(2)}, u32[]{:S(2)}) collective-permute-start(bf16[384,512]{1,0:T(8,128)(2,1)S(1)} %copy-done.2), channel_id=1, source_target_pairs={{0,8},{1,9},{2,10},{3,11},{4,12},{5,13},{6,14},{7,15},{8,0},{9,1},... | collective-permute-start | bytes 1179656 | tf_op jit(solution)/shard_map/ppermute | solution.py:77
  76.8 5.6 %collective-permute-done.22 = f16[512,512]{1,0:T(8,128)(2,1)S(1)} collective-permute-done((f16[512,512]{1,0:T(8,128)(2,1)S(1)}, f16[512,512]{1,0:T(8,128)(2,1)S(1)}, u32[]{:S(2)}, u32[]{:S(2)}) %collective-permute-start.22) | collective-permute-done | bytes 524320 | tf_op jit(solution)/shard_map/ppermute | solution.py:175
  85.0 2.8 %collective-permute-start.26 = (f32[2,32,512]{2,1,0:T(8,128)S(1)}, f32[2,32,512]{2,1,0:T(8,128)S(1)}, u32[]{:S(2)}, u32[]{:S(2)}) collective-permute-start(f32[2,32,512]{2,1,0:T(8,128)S(1)} %bitcast.141), channel_id=1, source_target_pairs={{0,64},{16,80},{32,96},{48,112},{64,0},{80,16},{96,32},{112,48},{1... | collective-permute-start | bytes 393224 | tf_op jit(solution)/shard_map/ppermute | solution.py:91
  92.6 4.8 %collective-permute-done.27 = f32[2,2,32,512]{3,2,0,1:T(8,128)S(1)} collective-permute-done((f32[2,2,32,512]{3,2,0,1:T(8,128)S(1)}, f32[2,2,32,512]{3,2,0,1:T(8,128)S(1)}, u32[]{:S(2)}, u32[]{:S(2)}) %collective-permute-start.27) | collective-permute-done | bytes 262176 | tf_op jit(solution)/shard_map/ppermute | solution.py:91
  97.5 10.1 %collective-permute-start.28 = (f32[2,2,2,32,512]{4,3,0,1,2:T(8,128)S(1)}, f32[2,2,2,32,512]{4,3,0,1,2:T(8,128)S(1)}, u32[]{:S(2)}, u32[]{:S(2)}) collective-permute-start(f32[2,2,2,32,512]{4,3,0,1,2:T(8,128)S(1)} %pad_maximum_fusion.1), channel_id=1, source_target_pairs={{0,16},{16,0},{32,48},{48,32},{64,80},{80,64},{96,112},{112,96},{1... | collective-permute-start | bytes 1572872 | tf_op jit(solution)/shard_map/ppermute | solution.py:91
  108.1 1.4 %fusion.27 = f32[512,512]{1,0:T(8,128)} fusion(f16[512,512]{1,0:T(8,128)(2,1)S(1)} %collective-permute-done.30, f16[512,512]{1,0:T(8,128)(2,1)S(1)} %collective-permute-done.29, f32[512,512]{1,0:T(8,128)S(1)} %fusion.51, f32[512,512]{1,0:T(8,128)S(1)} %fusion.52), kind=kLoop, calls=%fused_computation.51 | loop fusion | flops 2883584 | bytes 4194304 | tf_op jit(solution)/shard_map/add | solution.py:167
  109.9 1.3 %copy.21 = f32[512,512]{1,0:T(8,128)} copy(f32[512,512]{0,1:T(8,128)S(1)} %bitcast.131) | data formatting | bytes 2097152
  111.2 2.0 %add_convert_fusion = bf16[384,512]{1,0:T(8,128)(2,1)} fusion(f32[384,512]{1,0:T(8,128)S(1)} %fusion.7, f32[384,512]{1,0:T(8,128)} %collective-permute-done.24), kind=kLoop, calls=%fused_computation.54 | loop fusion | flops 393216 | bytes 1966080 | tf_op jit(solution)/shard_map/convert_element_type | solution.py:251
  (112 shorter events, 23.1 us)
Async XLA Ops:
  0.6 18.1 %collective-permute-start = (bf16[384,512]{1,0:T(8,128)(2,1)}, bf16[384,512]{1,0:T(8,128)(2,1)S(1)}, u32[]{:S(2)}, u32[]{:S(2)}) collective-permute-start(bf16[384,512]{1,0:T(8,128)(2,1)} %bitcast.120), channel_id=1, source_target_pairs={{0,8},{1,9},{2,10},{3,11},{4,12},{5,13},{6,14},{7,15},{8,0},{9,1},... | collective-permute-start | bytes 1179656 | tf_op jit(solution)/shard_map/ppermute | solution.py:77
  6.4 17.0 %collective-permute-start.2 = (bf16[512,512]{1,0:T(8,128)(2,1)S(1)}, bf16[512,512]{1,0:T(8,128)(2,1)S(1)}, u32[]{:S(2)}, u32[]{:S(2)}) collective-permute-start(bf16[512,512]{1,0:T(8,128)(2,1)S(1)} %bitcast.132), channel_id=1, source_target_pairs={{0,1},{1,2},{2,3},{3,4},{4,5},{5,6},{6,7},{7,0},{8,9},{9,10},{10,1... | collective-permute-start | bytes 1572872 | tf_op jit(solution)/shard_map/ppermute | solution.py:101
  8.1 15.3 %collective-permute-start.1 = (bf16[512,512]{1,0:T(8,128)(2,1)S(1)}, bf16[512,512]{1,0:T(8,128)(2,1)S(1)}, u32[]{:S(2)}, u32[]{:S(2)}) collective-permute-start(bf16[512,512]{1,0:T(8,128)(2,1)S(1)} %bitcast.133), channel_id=1, source_target_pairs={{0,7},{1,0},{2,1},{3,2},{4,3},{5,4},{6,5},{7,6},{8,15},{9,8},{10,9... | collective-permute-start | bytes 1572872 | tf_op jit(solution)/shard_map/ppermute | solution.py:101
  12.2 14.4 %collective-permute-start.5 = (bf16[384,512]{1,0:T(8,128)(2,1)}, bf16[384,512]{1,0:T(8,128)(2,1)S(1)}, u32[]{:S(2)}, u32[]{:S(2)}) collective-permute-start(bf16[384,512]{1,0:T(8,128)(2,1)} %get-tuple-element.228), channel_id=1, source_target_pairs={{0,8},{1,9},{2,10},{3,11},{4,12},{5,13},{6,14},{7,15},{8,0},{9,1},... | collective-permute-start | bytes 1179656 | tf_op jit(solution)/shard_map/ppermute | solution.py:77
  13.6 13.9 %collective-permute-start.4 = (bf16[2,2,2,32,512]{4,3,2,1,0:T(8,128)(2,1)S(1)}, bf16[2,2,2,32,512]{4,3,2,1,0:T(8,128)(2,1)}, u32[]{:S(2)}, u32[]{:S(2)}) collective-permute-start(bf16[2,2,2,32,512]{4,3,2,1,0:T(8,128)(2,1)S(1)} %dynamic-slice_bitcast_fusion.1), channel_id=1, source_target_pairs={{0,16},{16,0},{32,48},{48,32},{64,80},{80,64},{96,112},{112,96},{1... | collective-permute-start | bytes 786440 | tf_op jit(solution)/shard_map/ppermute | solution.py:85
  20.8 10.8 %collective-permute-start.9 = (bf16[384,512]{1,0:T(8,128)(2,1)S(1)}, bf16[384,512]{1,0:T(8,128)(2,1)S(1)}, u32[]{:S(2)}, u32[]{:S(2)}) collective-permute-start(bf16[384,512]{1,0:T(8,128)(2,1)S(1)} %copy-done.8), channel_id=1, source_target_pairs={{0,8},{1,9},{2,10},{3,11},{4,12},{5,13},{6,14},{7,15},{8,0},{9,1},... | collective-permute-start | bytes 1179656 | tf_op jit(solution)/shard_map/ppermute | solution.py:77
  23.4 13.1 %collective-permute-start.8 = (bf16[512,512]{1,0:T(8,128)(2,1)S(1)}, bf16[512,512]{1,0:T(8,128)(2,1)S(1)}, u32[]{:S(2)}, u32[]{:S(2)}) collective-permute-start(bf16[512,512]{1,0:T(8,128)(2,1)S(1)} %collective-permute-done.2), channel_id=1, source_target_pairs={{0,1},{1,2},{2,3},{3,4},{4,5},{5,6},{6,7},{7,0},{8,9},{9,10},{10,1... | collective-permute-start | bytes 1572872 | tf_op jit(solution)/shard_map/ppermute | solution.py:101
  23.4 13.3 %collective-permute-start.7 = (bf16[512,512]{1,0:T(8,128)(2,1)S(1)}, bf16[512,512]{1,0:T(8,128)(2,1)S(1)}, u32[]{:S(2)}, u32[]{:S(2)}) collective-permute-start(bf16[512,512]{1,0:T(8,128)(2,1)S(1)} %collective-permute-done.1), channel_id=1, source_target_pairs={{0,7},{1,0},{2,1},{3,2},{4,3},{5,4},{6,5},{7,6},{8,15},{9,8},{10,9... | collective-permute-start | bytes 1572872 | tf_op jit(solution)/shard_map/ppermute | solution.py:101
  29.5 9.9 %collective-permute-start.3 = (bf16[384,512]{1,0:T(8,128)(2,1)S(1)}, bf16[384,512]{1,0:T(8,128)(2,1)S(1)}, u32[]{:S(2)}, u32[]{:S(2)}) collective-permute-start(bf16[384,512]{1,0:T(8,128)(2,1)S(1)} %copy-done.7), channel_id=1, source_target_pairs={{0,8},{1,9},{2,10},{3,11},{4,12},{5,13},{6,14},{7,15},{8,0},{9,1},... | collective-permute-start | bytes 1179656 | tf_op jit(solution)/shard_map/ppermute | solution.py:77
  29.8 17.9 %collective-permute-start.11 = (f16[512,512]{1,0:T(8,128)(2,1)S(1)}, f16[512,512]{1,0:T(8,128)(2,1)S(1)}, u32[]{:S(2)}, u32[]{:S(2)}) collective-permute-start(f16[512,512]{1,0:T(8,128)(2,1)S(1)} %fusion.8), channel_id=1, source_target_pairs={{0,1},{1,2},{2,3},{3,4},{4,5},{5,6},{6,7},{7,0},{8,9},{9,10},{10,1... | collective-permute-start | bytes 1572872 | tf_op jit(solution)/shard_map/ppermute | solution.py:175
  31.6 7.3 %collective-permute-start.6 = (f32[2,2,32,512]{3,2,1,0:T(8,128)S(1)}, f32[2,2,32,512]{3,2,1,0:T(8,128)S(1)}, u32[]{:S(2)}, u32[]{:S(2)}) collective-permute-start(f32[2,2,32,512]{3,2,1,0:T(8,128)S(1)} %dynamic-slice_bitcast_fusion), channel_id=1, source_target_pairs={{0,32},{16,48},{32,0},{48,16},{64,96},{80,112},{96,64},{112,80},{1... | collective-permute-start | bytes 786440 | tf_op jit(solution)/shard_map/ppermute | solution.py:85
  33.6 21.0 %copy-start.9 = (f32[512,32]{0,1:T(8,128)S(1)}, f32[512,32]{0,1:T(8,128)}, u32[]{:S(2)}) copy-start(f32[512,32]{0,1:T(8,128)} %param.11) | copy-start | bytes 196612
  36.5 12.4 %collective-permute-start.10 = (bf16[384,512]{1,0:T(8,128)(2,1)S(1)}, bf16[384,512]{1,0:T(8,128)(2,1)S(1)}, u32[]{:S(2)}, u32[]{:S(2)}) collective-permute-start(bf16[384,512]{1,0:T(8,128)(2,1)S(1)} %copy-done.6), channel_id=1, source_target_pairs={{0,8},{1,9},{2,10},{3,11},{4,12},{5,13},{6,14},{7,15},{8,0},{9,1},... | collective-permute-start | bytes 1179656 | tf_op jit(solution)/shard_map/ppermute | solution.py:77
  36.7 12.6 %collective-permute-start.15 = (f16[512,512]{1,0:T(8,128)(2,1)S(1)}, f16[512,512]{1,0:T(8,128)(2,1)S(1)}, u32[]{:S(2)}, u32[]{:S(2)}) collective-permute-start(f16[512,512]{1,0:T(8,128)(2,1)S(1)} %fusion.9), channel_id=1, source_target_pairs={{0,7},{1,0},{2,1},{3,2},{4,3},{5,4},{6,5},{7,6},{8,15},{9,8},{10,9... | collective-permute-start | bytes 1572872 | tf_op jit(solution)/shard_map/ppermute | solution.py:175
  38.9 19.6 %collective-permute-start.12 = (bf16[384,512]{1,0:T(8,128)(2,1)S(1)}, bf16[384,512]{1,0:T(8,128)(2,1)S(1)}, u32[]{:S(2)}, u32[]{:S(2)}) collective-permute-start(bf16[384,512]{1,0:T(8,128)(2,1)S(1)} %copy-done.5), channel_id=1, source_target_pairs={{0,8},{1,9},{2,10},{3,11},{4,12},{5,13},{6,14},{7,15},{8,0},{9,1},... | collective-permute-start | bytes 1179656 | tf_op jit(solution)/shard_map/ppermute | solution.py:77
  39.5 19.0 %collective-permute-start.13 = (bf16[512,512]{1,0:T(8,128)(2,1)S(1)}, bf16[512,512]{1,0:T(8,128)(2,1)S(1)}, u32[]{:S(2)}, u32[]{:S(2)}) collective-permute-start(bf16[512,512]{1,0:T(8,128)(2,1)S(1)} %collective-permute-done.7), channel_id=1, source_target_pairs={{0,7},{1,0},{2,1},{3,2},{4,3},{5,4},{6,5},{7,6},{8,15},{9,8},{10,9... | collective-permute-start | bytes 1572872 | tf_op jit(solution)/shard_map/ppermute | solution.py:101
  48.4 15.7 %collective-permute-start.18 = (f16[512,512]{1,0:T(8,128)(2,1)S(1)}, f16[512,512]{1,0:T(8,128)(2,1)S(1)}, u32[]{:S(2)}, u32[]{:S(2)}) collective-permute-start(f16[512,512]{1,0:T(8,128)(2,1)S(1)} %fusion.12), channel_id=1, source_target_pairs={{0,1},{1,2},{2,3},{3,4},{4,5},{5,6},{6,7},{7,0},{8,9},{9,10},{10,1... | collective-permute-start | bytes 1572872 | tf_op jit(solution)/shard_map/ppermute | solution.py:175
  48.9 18.7 %collective-permute-start.16 = (bf16[384,512]{1,0:T(8,128)(2,1)S(1)}, bf16[384,512]{1,0:T(8,128)(2,1)S(1)}, u32[]{:S(2)}, u32[]{:S(2)}) collective-permute-start(bf16[384,512]{1,0:T(8,128)(2,1)S(1)} %copy-done.4), channel_id=1, source_target_pairs={{0,8},{1,9},{2,10},{3,11},{4,12},{5,13},{6,14},{7,15},{8,0},{9,1},... | collective-permute-start | bytes 1179656 | tf_op jit(solution)/shard_map/ppermute | solution.py:77
  49.2 5.4 %collective-permute-start.14 = (f32[2,32,512]{2,1,0:T(8,128)S(1)}, f32[2,32,512]{2,1,0:T(8,128)S(1)}, u32[]{:S(2)}, u32[]{:S(2)}) collective-permute-start(f32[2,32,512]{2,1,0:T(8,128)S(1)} %dynamic-slice_bitcast_fusion.2), channel_id=1, source_target_pairs={{0,64},{16,80},{32,96},{48,112},{64,0},{80,16},{96,32},{112,48},{1... | collective-permute-start | bytes 393224 | tf_op jit(solution)/shard_map/ppermute | solution.py:85
  54.6 17.8 %collective-permute-start.17 = (bf16[512,512]{1,0:T(8,128)(2,1)S(1)}, bf16[512,512]{1,0:T(8,128)(2,1)S(1)}, u32[]{:S(2)}, u32[]{:S(2)}) collective-permute-start(bf16[512,512]{1,0:T(8,128)(2,1)S(1)} %collective-permute-done.8), channel_id=1, source_target_pairs={{0,1},{1,2},{2,3},{3,4},{4,5},{5,6},{6,7},{7,0},{8,9},{9,10},{10,1... | collective-permute-start | bytes 1572872 | tf_op jit(solution)/shard_map/ppermute | solution.py:101
  58.5 17.2 %collective-permute-start.20 = (bf16[384,512]{1,0:T(8,128)(2,1)S(1)}, bf16[384,512]{1,0:T(8,128)(2,1)S(1)}, u32[]{:S(2)}, u32[]{:S(2)}) collective-permute-start(bf16[384,512]{1,0:T(8,128)(2,1)S(1)} %copy-done.3), channel_id=1, source_target_pairs={{0,8},{1,9},{2,10},{3,11},{4,12},{5,13},{6,14},{7,15},{8,0},{9,1},... | collective-permute-start | bytes 1179656 | tf_op jit(solution)/shard_map/ppermute | solution.py:77
  58.5 9.7 %collective-permute-start.19 = (f16[512,512]{1,0:T(8,128)(2,1)S(1)}, f16[512,512]{1,0:T(8,128)(2,1)S(1)}, u32[]{:S(2)}, u32[]{:S(2)}) collective-permute-start(f16[512,512]{1,0:T(8,128)(2,1)S(1)} %fusion.15), channel_id=1, source_target_pairs={{0,7},{1,0},{2,1},{3,2},{4,3},{5,4},{6,5},{7,6},{8,15},{9,8},{10,9... | collective-permute-start | bytes 1572872 | tf_op jit(solution)/shard_map/ppermute | solution.py:175
  64.1 20.8 %collective-permute-start.25 = (f32[96,512]{1,0:T(8,128)S(1)}, f32[96,512]{1,0:T(8,128)S(1)}, u32[]{:S(2)}, u32[]{:S(2)}) collective-permute-start(f32[96,512]{1,0:T(8,128)S(1)} %pad_maximum_fusion.3), channel_id=1, source_target_pairs={{0,128},{16,144},{32,160},{48,176},{64,192},{80,208},{96,224},{112... | collective-permute-start | bytes 589832 | tf_op jit(solution)/shard_map/ppermute | solution.py:91
  67.6 14.8 %collective-permute-start.22 = (f16[512,512]{1,0:T(8,128)(2,1)S(1)}, f16[512,512]{1,0:T(8,128)(2,1)S(1)}, u32[]{:S(2)}, u32[]{:S(2)}) collective-permute-start(f16[512,512]{1,0:T(8,128)(2,1)S(1)} %fusion.18), channel_id=1, source_target_pairs={{0,1},{1,2},{2,3},{3,4},{4,5},{5,6},{6,7},{7,0},{8,9},{9,10},{10,1... | collective-permute-start | bytes 1572872 | tf_op jit(solution)/shard_map/ppermute | solution.py:175
  68.2 15.0 %collective-permute-start.21 = (bf16[512,512]{1,0:T(8,128)(2,1)S(1)}, bf16[512,512]{1,0:T(8,128)(2,1)S(1)}, u32[]{:S(2)}, u32[]{:S(2)}) collective-permute-start(bf16[512,512]{1,0:T(8,128)(2,1)S(1)} %collective-permute-done.13), channel_id=1, source_target_pairs={{0,7},{1,0},{2,1},{3,2},{4,3},{5,4},{6,5},{7,6},{8,15},{9,8},{10,9... | collective-permute-start | bytes 1572872 | tf_op jit(solution)/shard_map/ppermute | solution.py:101
  72.4 11.5 %collective-permute-start.23 = (bf16[384,512]{1,0:T(8,128)(2,1)S(1)}, bf16[384,512]{1,0:T(8,128)(2,1)S(1)}, u32[]{:S(2)}, u32[]{:S(2)}) collective-permute-start(bf16[384,512]{1,0:T(8,128)(2,1)S(1)} %copy-done.2), channel_id=1, source_target_pairs={{0,8},{1,9},{2,10},{3,11},{4,12},{5,13},{6,14},{7,15},{8,0},{9,1},... | collective-permute-start | bytes 1179656 | tf_op jit(solution)/shard_map/ppermute | solution.py:77
  75.7 32.4 %collective-permute-start.30 = (f16[512,512]{1,0:T(8,128)(2,1)S(1)}, f16[512,512]{1,0:T(8,128)(2,1)S(1)}, u32[]{:S(2)}, u32[]{:S(2)}) collective-permute-start(f16[512,512]{1,0:T(8,128)(2,1)S(1)} %fusion.21), channel_id=1, source_target_pairs={{0,7},{1,0},{2,1},{3,2},{4,3},{5,4},{6,5},{7,6},{8,15},{9,8},{10,9... | collective-permute-start | bytes 1572872 | tf_op jit(solution)/shard_map/ppermute | solution.py:175
  83.1 25.1 %collective-permute-start.29 = (f16[512,512]{1,0:T(8,128)(2,1)S(1)}, f16[512,512]{1,0:T(8,128)(2,1)S(1)}, u32[]{:S(2)}, u32[]{:S(2)}) collective-permute-start(f16[512,512]{1,0:T(8,128)(2,1)S(1)} %fusion.24), channel_id=1, source_target_pairs={{0,1},{1,2},{2,3},{3,4},{4,5},{5,6},{6,7},{7,0},{8,9},{9,10},{10,1... | collective-permute-start | bytes 1572872 | tf_op jit(solution)/shard_map/ppermute | solution.py:175
  84.3 26.8 %collective-permute-start.24 = (f32[384,512]{1,0:T(8,128)S(1)}, f32[384,512]{1,0:T(8,128)}, u32[]{:S(2)}, u32[]{:S(2)}) collective-permute-start(f32[384,512]{1,0:T(8,128)S(1)} %convolution_add_fusion.5), channel_id=1, source_target_pairs={{0,8},{1,9},{2,10},{3,11},{4,12},{5,13},{6,14},{7,15},{8,0},{9,1},... | collective-permute-start | bytes 2359304 | tf_op jit(solution)/shard_map/ppermute | solution.py:77
  85.0 6.7 %collective-permute-start.26 = (f32[2,32,512]{2,1,0:T(8,128)S(1)}, f32[2,32,512]{2,1,0:T(8,128)S(1)}, u32[]{:S(2)}, u32[]{:S(2)}) collective-permute-start(f32[2,32,512]{2,1,0:T(8,128)S(1)} %bitcast.141), channel_id=1, source_target_pairs={{0,64},{16,80},{32,96},{48,112},{64,0},{80,16},{96,32},{112,48},{1... | collective-permute-start | bytes 393224 | tf_op jit(solution)/shard_map/ppermute | solution.py:91
  91.7 5.7 %collective-permute-start.27 = (f32[2,2,32,512]{3,2,0,1:T(8,128)S(1)}, f32[2,2,32,512]{3,2,0,1:T(8,128)S(1)}, u32[]{:S(2)}, u32[]{:S(2)}) collective-permute-start(f32[2,2,32,512]{3,2,0,1:T(8,128)S(1)} %pad_maximum_fusion.2), channel_id=1, source_target_pairs={{0,32},{16,48},{32,0},{48,16},{64,96},{80,112},{96,64},{112,80},{1... | collective-permute-start | bytes 786440 | tf_op jit(solution)/shard_map/ppermute | solution.py:91
  97.5 12.0 %collective-permute-start.28 = (f32[2,2,2,32,512]{4,3,0,1,2:T(8,128)S(1)}, f32[2,2,2,32,512]{4,3,0,1,2:T(8,128)S(1)}, u32[]{:S(2)}, u32[]{:S(2)}) collective-permute-start(f32[2,2,2,32,512]{4,3,0,1,2:T(8,128)S(1)} %pad_maximum_fusion.1), channel_id=1, source_target_pairs={{0,16},{16,0},{32,48},{48,32},{64,80},{80,64},{96,112},{112,96},{1... | collective-permute-start | bytes 1572872 | tf_op jit(solution)/shard_map/ppermute | solution.py:91
  (9 other events, 107.3 us)

commit v4 on v3

--- a/solution.py
+++ b/solution.py
@@ -229,6 +229,8 @@
     partner = theirs((2, 3, 4), None)
     own_dots(4)
     ring(4)
+    w[-3] = order.gate(w[-3])
+    order.done(w[-3])
     own_dots(5)
     ring(5)
     own_dots(6)

time: 113 us -> 113 us (level)
  starting transfers between devices: 50.7 us -> 46.7 us
  waiting for transfers between devices: 26.3 us -> 29.9 us
    ppermute x7, waiting for transfers between devices: 7.81 us -> 12.5 us  [w_hop(): lax.ppermute(w[-way * (h - 1)], 'fsdp', UP if way > 0 else DOWN)]
    ppermute x10, starting transfers between devices: 8.11 us -> 5.88 us  [over_y(): return lax.ppermute(x, 'fsdp', PAIR)]
  transfers between devices with their start and end apart: 31 -> 31, of which waited for: 8 -> 9; matrix products, arithmetic and copies ran while one was open for 29% -> 29% of each run, Pallas kernels for 0% -> 0%
where the time goes in v4:
time: 113 us
  starting transfers between devices  46.7 us (41%)
  waiting for transfers between devices  29.9 us (26%)
  matrix products  14.4 us (13%)
  local copies, waits for them, and re-layouts  12.5 us (11%)
  other arithmetic  8.03 us (7%)
  between operations  1.21 us (1%)
    ppermute x4, starting transfers between devices, spread_send(): return lax.ppermute(full, 'island', xor(1 << b))  14.9 us
    ppermute x7, starting transfers between devices, w_hop(): lax.ppermute(w[-way * (h - 1)], 'fsdp', UP if way > 0 else DOWN)  14.4 us
    ppermute x7, waiting for transfers between devices, w_hop(): lax.ppermute(w[-way * (h - 1)], 'fsdp', UP if way > 0 else DOWN)  12.5 us
    ppermute x7, waiting for transfers between devices, ring(): carry[way] = lax.ppermute(g, 'fsdp', UP if way > 0 else DOWN)  9.18 us
    dot_general x16, matrix products, tn(): lax.dot_general(a, b, (((0,), (0,)), ((), ())), preferred_element_type=f32)  8.34 us
    dot_general x16, matrix products, products(): d = jnp.dot(got, rows_w, preferred_element_type=f32)  6.1 us
    ppermute x7, starting transfers between devices, ring(): carry[way] = lax.ppermute(g, 'fsdp', UP if way > 0 else DOWN)  5.97 us
    ppermute x10, starting transfers between devices, over_y(): return lax.ppermute(x, 'fsdp', PAIR)  5.88 us
  transfers between devices with their start and end apart: 31, of which 9 were waited for; matrix products, arithmetic and copies ran while one was open for 29% of the time, Pallas kernels for 0%

profile of v4, /device:TPU:1, one launch (start us, length us, event | category | flops | bytes accessed | tf_op | source)
XLA Modules:
  0.0 112.8 jit_solution(13556282636946491994)
XLA Ops:
  0.6 2.2 %collective-permute-start = (bf16[384,512]{1,0:T(8,128)(2,1)}, bf16[384,512]{1,0:T(8,128)(2,1)S(1)}, u32[]{:S(2)}, u32[]{:S(2)}) collective-permute-start(bf16[384,512]{1,0:T(8,128)(2,1)} %bitcast.120), channel_id=1, source_target_pairs={{0,8},{1,9},{2,10},{3,11},{4,12},{5,13},{6,14},{7,15},{8,0},{9,1},... | collective-permute-start | bytes 1179656 | tf_op jit(solution)/shard_map/ppermute | solution.py:77
  2.9 3.6 %constant_dynamic-slice_fusion.9 = (bf16[384,512]{1,0:T(8,128)(2,1)}, bf16[384,512]{1,0:T(8,128)(2,1)}, bf16[384,512]{1,0:T(8,128)(2,1)}, bf16[384,512]{1,0:T(8,...) fusion(bf16[384,8192]{1,0:T(8,128)(2,1)} %bitcast.129, ...), kind=kLoop, calls=%fused_computation.86 | loop fusion | bytes 6291488 | tf_op jit(solution)/shard_map/dynamic_slice | solution.py:71
  6.4 1.7 %collective-permute-start.2 = (bf16[512,512]{1,0:T(8,128)(2,1)S(1)}, bf16[512,512]{1,0:T(8,128)(2,1)S(1)}, u32[]{:S(2)}, u32[]{:S(2)}) collective-permute-start(bf16[512,512]{1,0:T(8,128)(2,1)S(1)} %bitcast.132), channel_id=1, source_target_pairs={{0,1},{1,2},{2,3},{3,4},{4,5},{5,6},{6,7},{7,0},{8,9},{9,10},{10,1... | collective-permute-start | bytes 1572872 | tf_op jit(solution)/shard_map/ppermute | solution.py:101
  8.1 4.0 %collective-permute-start.1 = (bf16[512,512]{1,0:T(8,128)(2,1)S(1)}, bf16[512,512]{1,0:T(8,128)(2,1)S(1)}, u32[]{:S(2)}, u32[]{:S(2)}) collective-permute-start(bf16[512,512]{1,0:T(8,128)(2,1)S(1)} %bitcast.133), channel_id=1, source_target_pairs={{0,7},{1,0},{2,1},{3,2},{4,3},{5,4},{6,5},{7,6},{8,15},{9,8},{10,9... | collective-permute-start | bytes 1572872 | tf_op jit(solution)/shard_map/ppermute | solution.py:101
  12.3 1.3 %copy.18 = bf16[1,512,512]{1,2,0:T(8,128)(2,1)S(1)} copy(bf16[1,512,512]{2,1,0:T(8,128)(2,1)} %param.9) | data formatting | bytes 1048576 | tf_op args[3]
  13.6 1.6 %collective-permute-start.4 = (bf16[2,2,2,32,512]{4,3,2,1,0:T(8,128)(2,1)S(1)}, bf16[2,2,2,32,512]{4,3,2,1,0:T(8,128)(2,1)}, u32[]{:S(2)}, u32[]{:S(2)}) collective-permute-start(bf16[2,2,2,32,512]{4,3,2,1,0:T(8,128)(2,1)S(1)} %dynamic-slice_bitcast_fusion.1), channel_id=1, source_target_pairs={{0,16},{16,0},{32,48},{48,32},{64,80},{80,64},{96,112},{112,96},{1... | collective-permute-start | bytes 786440 | tf_op jit(solution)/shard_map/ppermute | solution.py:85
  15.2 2.5 %copy.19 = f32[512,512]{0,1:T(8,128)} copy(f32[512,512]{1,0:T(8,128)} %param.10) | data formatting | bytes 2097152 | tf_op args[4]
  18.7 2.1 %constant_dynamic-slice_fusion.1 = (bf16[384,512]{1,0:T(8,128)(2,1)S(1)}, bf16[384,512]{1,0:T(8,128)(2,1)S(1)}, bf16[384,512]{1,0:T(8,128)(2,1)S(1)}, bf16[384,5...) fusion(bf16[384,8192]{1,0:T(8,128)(2,1)} %bitcast.130, ...), kind=kLoop, calls=%fused_computation.78 | loop fusion | bytes 6291488 | tf_op jit(solution)/shard_map/dynamic_slice | solution.py:71
  20.8 1.4 %collective-permute-start.9 = (bf16[384,512]{1,0:T(8,128)(2,1)S(1)}, bf16[384,512]{1,0:T(8,128)(2,1)S(1)}, u32[]{:S(2)}, u32[]{:S(2)}) collective-permute-start(bf16[384,512]{1,0:T(8,128)(2,1)S(1)} %copy-done.8), channel_id=1, source_target_pairs={{0,8},{1,9},{2,10},{3,11},{4,12},{5,13},{6,14},{7,15},{8,0},{9,1},... | collective-permute-start | bytes 1179656 | tf_op jit(solution)/shard_map/ppermute | solution.py:77
  22.2 1.2 %collective-permute-done.2 = bf16[512,512]{1,0:T(8,128)(2,1)S(1)} collective-permute-done((bf16[512,512]{1,0:T(8,128)(2,1)S(1)}, bf16[512,512]{1,0:T(8,128)(2,1)S(1)}, u32[]{:S(2)}, u32[]{:S(2)}) %collective-permute-start.2) | collective-permute-done | bytes 524320 | tf_op jit(solution)/shard_map/ppermute | solution.py:101
  23.4 2.7 %collective-permute-start.7 = (bf16[512,512]{1,0:T(8,128)(2,1)S(1)}, bf16[512,512]{1,0:T(8,128)(2,1)S(1)}, u32[]{:S(2)}, u32[]{:S(2)}) collective-permute-start(bf16[512,512]{1,0:T(8,128)(2,1)S(1)} %collective-permute-done.1), channel_id=1, source_target_pairs={{0,7},{1,0},{2,1},{3,2},{4,3},{5,4},{6,5},{7,6},{8,15},{9,8},{10,9... | collective-permute-start | bytes 1572872 | tf_op jit(solution)/shard_map/ppermute | solution.py:101
  27.6 1.0 convert_add_fusion
  29.8 1.8 %collective-permute-done.9 = bf16[384,512]{1,0:T(8,128)(2,1)S(1)} collective-permute-done((bf16[384,512]{1,0:T(8,128)(2,1)S(1)}, bf16[384,512]{1,0:T(8,128)(2,1)S(1)}, u32[]{:S(2)}, u32[]{:S(2)}) %collective-permute-start.9) | collective-permute-done | bytes 393248 | tf_op jit(solution)/shard_map/ppermute | solution.py:77
  31.6 1.2 %collective-permute-start.6 = (f32[2,2,32,512]{3,2,1,0:T(8,128)S(1)}, f32[2,2,32,512]{3,2,1,0:T(8,128)S(1)}, u32[]{:S(2)}, u32[]{:S(2)}) collective-permute-start(f32[2,2,32,512]{3,2,1,0:T(8,128)S(1)} %dynamic-slice_bitcast_fusion), channel_id=1, source_target_pairs={{0,32},{16,48},{32,0},{48,16},{64,96},{80,112},{96,64},{112,80},{1... | collective-permute-start | bytes 786440 | tf_op jit(solution)/shard_map/ppermute | solution.py:85
  33.7 2.8 %collective-permute-done.8 = bf16[512,512]{1,0:T(8,128)(2,1)S(1)} collective-permute-done((bf16[512,512]{1,0:T(8,128)(2,1)S(1)}, bf16[512,512]{1,0:T(8,128)(2,1)S(1)}, u32[]{:S(2)}, u32[]{:S(2)}) %collective-permute-start.8) | collective-permute-done | bytes 524320 | tf_op jit(solution)/shard_map/ppermute | solution.py:101
  36.7 2.2 %collective-permute-start.15 = (f16[512,512]{1,0:T(8,128)(2,1)S(1)}, f16[512,512]{1,0:T(8,128)(2,1)S(1)}, u32[]{:S(2)}, u32[]{:S(2)}) collective-permute-start(f16[512,512]{1,0:T(8,128)(2,1)S(1)} %fusion.9), channel_id=1, source_target_pairs={{0,7},{1,0},{2,1},{3,2},{4,3},{5,4},{6,5},{7,6},{8,15},{9,8},{10,9... | collective-permute-start | bytes 1572872 | tf_op jit(solution)/shard_map/ppermute | solution.py:175
  39.5 3.1 %collective-permute-start.13 = (bf16[512,512]{1,0:T(8,128)(2,1)S(1)}, bf16[512,512]{1,0:T(8,128)(2,1)S(1)}, u32[]{:S(2)}, u32[]{:S(2)}) collective-permute-start(bf16[512,512]{1,0:T(8,128)(2,1)S(1)} %collective-permute-done.7), channel_id=1, source_target_pairs={{0,7},{1,0},{2,1},{3,2},{4,3},{5,4},{6,5},{7,6},{8,15},{9,8},{10,9... | collective-permute-start | bytes 1572872 | tf_op jit(solution)/shard_map/ppermute | solution.py:101
  43.1 4.6 %collective-permute-done.11 = f16[512,512]{1,0:T(8,128)(2,1)S(1)} collective-permute-done((f16[512,512]{1,0:T(8,128)(2,1)S(1)}, f16[512,512]{1,0:T(8,128)(2,1)S(1)}, u32[]{:S(2)}, u32[]{:S(2)}) %collective-permute-start.11) | collective-permute-done | bytes 524320 | tf_op jit(solution)/shard_map/ppermute | solution.py:175
  49.1 2.8 %collective-permute-start.14 = (f32[2,32,512]{2,1,0:T(8,128)S(1)}, f32[2,32,512]{2,1,0:T(8,128)S(1)}, u32[]{:S(2)}, u32[]{:S(2)}) collective-permute-start(f32[2,32,512]{2,1,0:T(8,128)S(1)} %dynamic-slice_bitcast_fusion.2), channel_id=1, source_target_pairs={{0,64},{16,80},{32,96},{48,112},{64,0},{80,16},{96,32},{112,48},{1... | collective-permute-start | bytes 393224 | tf_op jit(solution)/shard_map/ppermute | solution.py:85
  52.9 1.6 %collective-permute-done.14 = f32[2,32,512]{2,1,0:T(8,128)S(1)} collective-permute-done((f32[2,32,512]{2,1,0:T(8,128)S(1)}, f32[2,32,512]{2,1,0:T(8,128)S(1)}, u32[]{:S(2)}, u32[]{:S(2)}) %collective-permute-start.14) | collective-permute-done | bytes 131104 | tf_op jit(solution)/shard_map/ppermute | solution.py:85
  54.7 3.8 %collective-permute-done.13 = bf16[512,512]{1,0:T(8,128)(2,1)S(1)} collective-permute-done((bf16[512,512]{1,0:T(8,128)(2,1)S(1)}, bf16[512,512]{1,0:T(8,128)(2,1)S(1)}, u32[]{:S(2)}, u32[]{:S(2)}) %collective-permute-start.13) | collective-permute-done | bytes 524320 | tf_op jit(solution)/shard_map/ppermute | solution.py:101
  58.5 3.5 %collective-permute-start.19 = (f16[512,512]{1,0:T(8,128)(2,1)S(1)}, f16[512,512]{1,0:T(8,128)(2,1)S(1)}, u32[]{:S(2)}, u32[]{:S(2)}) collective-permute-start(f16[512,512]{1,0:T(8,128)(2,1)S(1)} %fusion.15), channel_id=1, source_target_pairs={{0,7},{1,0},{2,1},{3,2},{4,3},{5,4},{6,5},{7,6},{8,15},{9,8},{10,9... | collective-permute-start | bytes 1572872 | tf_op jit(solution)/shard_map/ppermute | solution.py:175
  64.1 2.4 %collective-permute-start.25 = (f32[96,512]{1,0:T(8,128)S(1)}, f32[96,512]{1,0:T(8,128)S(1)}, u32[]{:S(2)}, u32[]{:S(2)}) collective-permute-start(f32[96,512]{1,0:T(8,128)S(1)} %pad_maximum_fusion.3), channel_id=1, source_target_pairs={{0,128},{16,144},{32,160},{48,176},{64,192},{80,208},{96,224},{112... | collective-permute-start | bytes 589832 | tf_op jit(solution)/shard_map/ppermute | solution.py:91
  67.1 4.7 %collective-permute-done.17 = bf16[512,512]{1,0:T(8,128)(2,1)S(1)} collective-permute-done((bf16[512,512]{1,0:T(8,128)(2,1)S(1)}, bf16[512,512]{1,0:T(8,128)(2,1)S(1)}, u32[]{:S(2)}, u32[]{:S(2)}) %collective-permute-start.17) | collective-permute-done | bytes 524320 | tf_op jit(solution)/shard_map/ppermute | solution.py:101
  72.3 2.7 %collective-permute-start.21 = (bf16[512,512]{1,0:T(8,128)(2,1)S(1)}, bf16[512,512]{1,0:T(8,128)(2,1)S(1)}, u32[]{:S(2)}, u32[]{:S(2)}) collective-permute-start(bf16[512,512]{1,0:T(8,128)(2,1)S(1)} %collective-permute-done.13), channel_id=1, source_target_pairs={{0,7},{1,0},{2,1},{3,2},{4,3},{5,4},{6,5},{7,6},{8,15},{9,8},{10,9... | collective-permute-start | bytes 1572872 | tf_op jit(solution)/shard_map/ppermute | solution.py:101
  78.5 4.5 %collective-permute-done.22 = f16[512,512]{1,0:T(8,128)(2,1)S(1)} collective-permute-done((f16[512,512]{1,0:T(8,128)(2,1)S(1)}, f16[512,512]{1,0:T(8,128)(2,1)S(1)}, u32[]{:S(2)}, u32[]{:S(2)}) %collective-permute-start.22) | collective-permute-done | bytes 524320 | tf_op jit(solution)/shard_map/ppermute | solution.py:175
  85.6 2.8 %collective-permute-start.26 = (f32[2,32,512]{2,1,0:T(8,128)S(1)}, f32[2,32,512]{2,1,0:T(8,128)S(1)}, u32[]{:S(2)}, u32[]{:S(2)}) collective-permute-start(f32[2,32,512]{2,1,0:T(8,128)S(1)} %bitcast.141), channel_id=1, source_target_pairs={{0,64},{16,80},{32,96},{48,112},{64,0},{80,16},{96,32},{112,48},{1... | collective-permute-start | bytes 393224 | tf_op jit(solution)/shard_map/ppermute | solution.py:91
  93.2 4.8 %collective-permute-done.27 = f32[2,2,32,512]{3,2,0,1:T(8,128)S(1)} collective-permute-done((f32[2,2,32,512]{3,2,0,1:T(8,128)S(1)}, f32[2,2,32,512]{3,2,0,1:T(8,128)S(1)}, u32[]{:S(2)}, u32[]{:S(2)}) %collective-permute-start.27) | collective-permute-done | bytes 262176 | tf_op jit(solution)/shard_map/ppermute | solution.py:91
  98.1 9.2 %collective-permute-start.28 = (f32[2,2,2,32,512]{4,3,0,1,2:T(8,128)S(1)}, f32[2,2,2,32,512]{4,3,0,1,2:T(8,128)S(1)}, u32[]{:S(2)}, u32[]{:S(2)}) collective-permute-start(f32[2,2,2,32,512]{4,3,0,1,2:T(8,128)S(1)} %pad_maximum_fusion.1), channel_id=1, source_target_pairs={{0,16},{16,0},{32,48},{48,32},{64,80},{80,64},{96,112},{112,96},{1... | collective-permute-start | bytes 1572872 | tf_op jit(solution)/shard_map/ppermute | solution.py:91
  107.8 1.4 %fusion.27 = f32[512,512]{1,0:T(8,128)} fusion(f16[512,512]{1,0:T(8,128)(2,1)S(1)} %collective-permute-done.30, f16[512,512]{1,0:T(8,128)(2,1)S(1)} %collective-permute-done.29, f32[512,512]{1,0:T(8,128)S(1)} %fusion.51, f32[512,512]{1,0:T(8,128)S(1)} %fusion.52), kind=kLoop, calls=%fused_computation.51 | loop fusion | flops 2883584 | bytes 4194304 | tf_op jit(solution)/shard_map/add | solution.py:167
  109.5 1.3 %copy.21 = f32[512,512]{1,0:T(8,128)} copy(f32[512,512]{0,1:T(8,128)S(1)} %bitcast.131) | data formatting | bytes 2097152
  110.9 2.0 %add_convert_fusion = bf16[384,512]{1,0:T(8,128)(2,1)} fusion(f32[384,512]{1,0:T(8,128)S(1)} %fusion.7, f32[384,512]{1,0:T(8,128)} %collective-permute-done.24), kind=kLoop, calls=%fused_computation.54 | loop fusion | flops 393216 | bytes 1966080 | tf_op jit(solution)/shard_map/convert_element_type | solution.py:253
  (112 shorter events, 22.9 us)
Async XLA Ops:
  0.6 18.1 %collective-permute-start = (bf16[384,512]{1,0:T(8,128)(2,1)}, bf16[384,512]{1,0:T(8,128)(2,1)S(1)}, u32[]{:S(2)}, u32[]{:S(2)}) collective-permute-start(bf16[384,512]{1,0:T(8,128)(2,1)} %bitcast.120), channel_id=1, source_target_pairs={{0,8},{1,9},{2,10},{3,11},{4,12},{5,13},{6,14},{7,15},{8,0},{9,1},... | collective-permute-start | bytes 1179656 | tf_op jit(solution)/shard_map/ppermute | solution.py:77
  6.4 17.0 %collective-permute-start.2 = (bf16[512,512]{1,0:T(8,128)(2,1)S(1)}, bf16[512,512]{1,0:T(8,128)(2,1)S(1)}, u32[]{:S(2)}, u32[]{:S(2)}) collective-permute-start(bf16[512,512]{1,0:T(8,128)(2,1)S(1)} %bitcast.132), channel_id=1, source_target_pairs={{0,1},{1,2},{2,3},{3,4},{4,5},{5,6},{6,7},{7,0},{8,9},{9,10},{10,1... | collective-permute-start | bytes 1572872 | tf_op jit(solution)/shard_map/ppermute | solution.py:101
  8.1 15.3 %collective-permute-start.1 = (bf16[512,512]{1,0:T(8,128)(2,1)S(1)}, bf16[512,512]{1,0:T(8,128)(2,1)S(1)}, u32[]{:S(2)}, u32[]{:S(2)}) collective-permute-start(bf16[512,512]{1,0:T(8,128)(2,1)S(1)} %bitcast.133), channel_id=1, source_target_pairs={{0,7},{1,0},{2,1},{3,2},{4,3},{5,4},{6,5},{7,6},{8,15},{9,8},{10,9... | collective-permute-start | bytes 1572872 | tf_op jit(solution)/shard_map/ppermute | solution.py:101
  12.2 14.4 %collective-permute-start.5 = (bf16[384,512]{1,0:T(8,128)(2,1)}, bf16[384,512]{1,0:T(8,128)(2,1)S(1)}, u32[]{:S(2)}, u32[]{:S(2)}) collective-permute-start(bf16[384,512]{1,0:T(8,128)(2,1)} %get-tuple-element.230), channel_id=1, source_target_pairs={{0,8},{1,9},{2,10},{3,11},{4,12},{5,13},{6,14},{7,15},{8,0},{9,1},... | collective-permute-start | bytes 1179656 | tf_op jit(solution)/shard_map/ppermute | solution.py:77
  13.6 13.9 %collective-permute-start.4 = (bf16[2,2,2,32,512]{4,3,2,1,0:T(8,128)(2,1)S(1)}, bf16[2,2,2,32,512]{4,3,2,1,0:T(8,128)(2,1)}, u32[]{:S(2)}, u32[]{:S(2)}) collective-permute-start(bf16[2,2,2,32,512]{4,3,2,1,0:T(8,128)(2,1)S(1)} %dynamic-slice_bitcast_fusion.1), channel_id=1, source_target_pairs={{0,16},{16,0},{32,48},{48,32},{64,80},{80,64},{96,112},{112,96},{1... | collective-permute-start | bytes 786440 | tf_op jit(solution)/shard_map/ppermute | solution.py:85
  20.8 10.8 %collective-permute-start.9 = (bf16[384,512]{1,0:T(8,128)(2,1)S(1)}, bf16[384,512]{1,0:T(8,128)(2,1)S(1)}, u32[]{:S(2)}, u32[]{:S(2)}) collective-permute-start(bf16[384,512]{1,0:T(8,128)(2,1)S(1)} %copy-done.8), channel_id=1, source_target_pairs={{0,8},{1,9},{2,10},{3,11},{4,12},{5,13},{6,14},{7,15},{8,0},{9,1},... | collective-permute-start | bytes 1179656 | tf_op jit(solution)/shard_map/ppermute | solution.py:77
  23.4 13.1 %collective-permute-start.8 = (bf16[512,512]{1,0:T(8,128)(2,1)S(1)}, bf16[512,512]{1,0:T(8,128)(2,1)S(1)}, u32[]{:S(2)}, u32[]{:S(2)}) collective-permute-start(bf16[512,512]{1,0:T(8,128)(2,1)S(1)} %collective-permute-done.2), channel_id=1, source_target_pairs={{0,1},{1,2},{2,3},{3,4},{4,5},{5,6},{6,7},{7,0},{8,9},{9,10},{10,1... | collective-permute-start | bytes 1572872 | tf_op jit(solution)/shard_map/ppermute | solution.py:101
  23.4 13.3 %collective-permute-start.7 = (bf16[512,512]{1,0:T(8,128)(2,1)S(1)}, bf16[512,512]{1,0:T(8,128)(2,1)S(1)}, u32[]{:S(2)}, u32[]{:S(2)}) collective-permute-start(bf16[512,512]{1,0:T(8,128)(2,1)S(1)} %collective-permute-done.1), channel_id=1, source_target_pairs={{0,7},{1,0},{2,1},{3,2},{4,3},{5,4},{6,5},{7,6},{8,15},{9,8},{10,9... | collective-permute-start | bytes 1572872 | tf_op jit(solution)/shard_map/ppermute | solution.py:101
  29.5 9.9 %collective-permute-start.3 = (bf16[384,512]{1,0:T(8,128)(2,1)S(1)}, bf16[384,512]{1,0:T(8,128)(2,1)S(1)}, u32[]{:S(2)}, u32[]{:S(2)}) collective-permute-start(bf16[384,512]{1,0:T(8,128)(2,1)S(1)} %copy-done.7), channel_id=1, source_target_pairs={{0,8},{1,9},{2,10},{3,11},{4,12},{5,13},{6,14},{7,15},{8,0},{9,1},... | collective-permute-start | bytes 1179656 | tf_op jit(solution)/shard_map/ppermute | solution.py:77
  29.8 17.9 %collective-permute-start.11 = (f16[512,512]{1,0:T(8,128)(2,1)S(1)}, f16[512,512]{1,0:T(8,128)(2,1)S(1)}, u32[]{:S(2)}, u32[]{:S(2)}) collective-permute-start(f16[512,512]{1,0:T(8,128)(2,1)S(1)} %fusion.8), channel_id=1, source_target_pairs={{0,1},{1,2},{2,3},{3,4},{4,5},{5,6},{6,7},{7,0},{8,9},{9,10},{10,1... | collective-permute-start | bytes 1572872 | tf_op jit(solution)/shard_map/ppermute | solution.py:175
  31.6 7.3 %collective-permute-start.6 = (f32[2,2,32,512]{3,2,1,0:T(8,128)S(1)}, f32[2,2,32,512]{3,2,1,0:T(8,128)S(1)}, u32[]{:S(2)}, u32[]{:S(2)}) collective-permute-start(f32[2,2,32,512]{3,2,1,0:T(8,128)S(1)} %dynamic-slice_bitcast_fusion), channel_id=1, source_target_pairs={{0,32},{16,48},{32,0},{48,16},{64,96},{80,112},{96,64},{112,80},{1... | collective-permute-start | bytes 786440 | tf_op jit(solution)/shard_map/ppermute | solution.py:85
  33.7 21.0 %copy-start.9 = (f32[512,32]{0,1:T(8,128)S(1)}, f32[512,32]{0,1:T(8,128)}, u32[]{:S(2)}) copy-start(f32[512,32]{0,1:T(8,128)} %param.11) | copy-start | bytes 196612
  36.5 12.4 %collective-permute-start.10 = (bf16[384,512]{1,0:T(8,128)(2,1)S(1)}, bf16[384,512]{1,0:T(8,128)(2,1)S(1)}, u32[]{:S(2)}, u32[]{:S(2)}) collective-permute-start(bf16[384,512]{1,0:T(8,128)(2,1)S(1)} %copy-done.6), channel_id=1, source_target_pairs={{0,8},{1,9},{2,10},{3,11},{4,12},{5,13},{6,14},{7,15},{8,0},{9,1},... | collective-permute-start | bytes 1179656 | tf_op jit(solution)/shard_map/ppermute | solution.py:77
  36.7 12.4 %collective-permute-start.15 = (f16[512,512]{1,0:T(8,128)(2,1)S(1)}, f16[512,512]{1,0:T(8,128)(2,1)S(1)}, u32[]{:S(2)}, u32[]{:S(2)}) collective-permute-start(f16[512,512]{1,0:T(8,128)(2,1)S(1)} %fusion.9), channel_id=1, source_target_pairs={{0,7},{1,0},{2,1},{3,2},{4,3},{5,4},{6,5},{7,6},{8,15},{9,8},{10,9... | collective-permute-start | bytes 1572872 | tf_op jit(solution)/shard_map/ppermute | solution.py:175
  38.9 19.6 %collective-permute-start.12 = (bf16[384,512]{1,0:T(8,128)(2,1)S(1)}, bf16[384,512]{1,0:T(8,128)(2,1)S(1)}, u32[]{:S(2)}, u32[]{:S(2)}) collective-permute-start(bf16[384,512]{1,0:T(8,128)(2,1)S(1)} %copy-done.5), channel_id=1, source_target_pairs={{0,8},{1,9},{2,10},{3,11},{4,12},{5,13},{6,14},{7,15},{8,0},{9,1},... | collective-permute-start | bytes 1179656 | tf_op jit(solution)/shard_map/ppermute | solution.py:77
  39.5 19.0 %collective-permute-start.13 = (bf16[512,512]{1,0:T(8,128)(2,1)S(1)}, bf16[512,512]{1,0:T(8,128)(2,1)S(1)}, u32[]{:S(2)}, u32[]{:S(2)}) collective-permute-start(bf16[512,512]{1,0:T(8,128)(2,1)S(1)} %collective-permute-done.7), channel_id=1, source_target_pairs={{0,7},{1,0},{2,1},{3,2},{4,3},{5,4},{6,5},{7,6},{8,15},{9,8},{10,9... | collective-permute-start | bytes 1572872 | tf_op jit(solution)/shard_map/ppermute | solution.py:101
  48.4 15.7 %collective-permute-start.18 = (f16[512,512]{1,0:T(8,128)(2,1)S(1)}, f16[512,512]{1,0:T(8,128)(2,1)S(1)}, u32[]{:S(2)}, u32[]{:S(2)}) collective-permute-start(f16[512,512]{1,0:T(8,128)(2,1)S(1)} %fusion.12), channel_id=1, source_target_pairs={{0,1},{1,2},{2,3},{3,4},{4,5},{5,6},{6,7},{7,0},{8,9},{9,10},{10,1... | collective-permute-start | bytes 1572872 | tf_op jit(solution)/shard_map/ppermute | solution.py:175
  48.9 22.9 %collective-permute-start.17 = (bf16[512,512]{1,0:T(8,128)(2,1)S(1)}, bf16[512,512]{1,0:T(8,128)(2,1)S(1)}, u32[]{:S(2)}, u32[]{:S(2)}) collective-permute-start(bf16[512,512]{1,0:T(8,128)(2,1)S(1)} %collective-permute-done.8), channel_id=1, source_target_pairs={{0,1},{1,2},{2,3},{3,4},{4,5},{5,6},{6,7},{7,0},{8,9},{9,10},{10,1... | collective-permute-start | bytes 1572872 | tf_op jit(solution)/shard_map/ppermute | solution.py:101
  49.1 5.4 %collective-permute-start.14 = (f32[2,32,512]{2,1,0:T(8,128)S(1)}, f32[2,32,512]{2,1,0:T(8,128)S(1)}, u32[]{:S(2)}, u32[]{:S(2)}) collective-permute-start(f32[2,32,512]{2,1,0:T(8,128)S(1)} %dynamic-slice_bitcast_fusion.2), channel_id=1, source_target_pairs={{0,64},{16,80},{32,96},{48,112},{64,0},{80,16},{96,32},{112,48},{1... | collective-permute-start | bytes 393224 | tf_op jit(solution)/shard_map/ppermute | solution.py:85
  54.5 17.8 %collective-permute-start.16 = (bf16[384,512]{1,0:T(8,128)(2,1)S(1)}, bf16[384,512]{1,0:T(8,128)(2,1)S(1)}, u32[]{:S(2)}, u32[]{:S(2)}) collective-permute-start(bf16[384,512]{1,0:T(8,128)(2,1)S(1)} %copy-done.4), channel_id=1, source_target_pairs={{0,8},{1,9},{2,10},{3,11},{4,12},{5,13},{6,14},{7,15},{8,0},{9,1},... | collective-permute-start | bytes 1179656 | tf_op jit(solution)/shard_map/ppermute | solution.py:77
  58.5 19.5 %collective-permute-start.20 = (bf16[384,512]{1,0:T(8,128)(2,1)S(1)}, bf16[384,512]{1,0:T(8,128)(2,1)S(1)}, u32[]{:S(2)}, u32[]{:S(2)}) collective-permute-start(bf16[384,512]{1,0:T(8,128)(2,1)S(1)} %copy-done.3), channel_id=1, source_target_pairs={{0,8},{1,9},{2,10},{3,11},{4,12},{5,13},{6,14},{7,15},{8,0},{9,1},... | collective-permute-start | bytes 1179656 | tf_op jit(solution)/shard_map/ppermute | solution.py:77
  58.5 17.0 %collective-permute-start.19 = (f16[512,512]{1,0:T(8,128)(2,1)S(1)}, f16[512,512]{1,0:T(8,128)(2,1)S(1)}, u32[]{:S(2)}, u32[]{:S(2)}) collective-permute-start(f16[512,512]{1,0:T(8,128)(2,1)S(1)} %fusion.15), channel_id=1, source_target_pairs={{0,7},{1,0},{2,1},{3,2},{4,3},{5,4},{6,5},{7,6},{8,15},{9,8},{10,9... | collective-permute-start | bytes 1572872 | tf_op jit(solution)/shard_map/ppermute | solution.py:175
  64.1 21.4 %collective-permute-start.25 = (f32[96,512]{1,0:T(8,128)S(1)}, f32[96,512]{1,0:T(8,128)S(1)}, u32[]{:S(2)}, u32[]{:S(2)}) collective-permute-start(f32[96,512]{1,0:T(8,128)S(1)} %pad_maximum_fusion.3), channel_id=1, source_target_pairs={{0,128},{16,144},{32,160},{48,176},{64,192},{80,208},{96,224},{112... | collective-permute-start | bytes 589832 | tf_op jit(solution)/shard_map/ppermute | solution.py:91
  71.8 11.2 %collective-permute-start.22 = (f16[512,512]{1,0:T(8,128)(2,1)S(1)}, f16[512,512]{1,0:T(8,128)(2,1)S(1)}, u32[]{:S(2)}, u32[]{:S(2)}) collective-permute-start(f16[512,512]{1,0:T(8,128)(2,1)S(1)} %fusion.18), channel_id=1, source_target_pairs={{0,1},{1,2},{2,3},{3,4},{4,5},{5,6},{6,7},{7,0},{8,9},{9,10},{10,1... | collective-permute-start | bytes 1572872 | tf_op jit(solution)/shard_map/ppermute | solution.py:175
  72.3 11.5 %collective-permute-start.21 = (bf16[512,512]{1,0:T(8,128)(2,1)S(1)}, bf16[512,512]{1,0:T(8,128)(2,1)S(1)}, u32[]{:S(2)}, u32[]{:S(2)}) collective-permute-start(bf16[512,512]{1,0:T(8,128)(2,1)S(1)} %collective-permute-done.13), channel_id=1, source_target_pairs={{0,7},{1,0},{2,1},{3,2},{4,3},{5,4},{6,5},{7,6},{8,15},{9,8},{10,9... | collective-permute-start | bytes 1572872 | tf_op jit(solution)/shard_map/ppermute | solution.py:101
  75.6 9.1 %collective-permute-start.23 = (bf16[384,512]{1,0:T(8,128)(2,1)S(1)}, bf16[384,512]{1,0:T(8,128)(2,1)S(1)}, u32[]{:S(2)}, u32[]{:S(2)}) collective-permute-start(bf16[384,512]{1,0:T(8,128)(2,1)S(1)} %copy-done.2), channel_id=1, source_target_pairs={{0,8},{1,9},{2,10},{3,11},{4,12},{5,13},{6,14},{7,15},{8,0},{9,1},... | collective-permute-start | bytes 1179656 | tf_op jit(solution)/shard_map/ppermute | solution.py:77
  78.0 29.8 %collective-permute-start.30 = (f16[512,512]{1,0:T(8,128)(2,1)S(1)}, f16[512,512]{1,0:T(8,128)(2,1)S(1)}, u32[]{:S(2)}, u32[]{:S(2)}) collective-permute-start(f16[512,512]{1,0:T(8,128)(2,1)S(1)} %fusion.21), channel_id=1, source_target_pairs={{0,7},{1,0},{2,1},{3,2},{4,3},{5,4},{6,5},{7,6},{8,15},{9,8},{10,9... | collective-permute-start | bytes 1572872 | tf_op jit(solution)/shard_map/ppermute | solution.py:175
  83.8 24.1 %collective-permute-start.29 = (f16[512,512]{1,0:T(8,128)(2,1)S(1)}, f16[512,512]{1,0:T(8,128)(2,1)S(1)}, u32[]{:S(2)}, u32[]{:S(2)}) collective-permute-start(f16[512,512]{1,0:T(8,128)(2,1)S(1)} %fusion.24), channel_id=1, source_target_pairs={{0,1},{1,2},{2,3},{3,4},{4,5},{5,6},{6,7},{7,0},{8,9},{9,10},{10,1... | collective-permute-start | bytes 1572872 | tf_op jit(solution)/shard_map/ppermute | solution.py:175
  85.0 25.9 %collective-permute-start.24 = (f32[384,512]{1,0:T(8,128)S(1)}, f32[384,512]{1,0:T(8,128)}, u32[]{:S(2)}, u32[]{:S(2)}) collective-permute-start(f32[384,512]{1,0:T(8,128)S(1)} %convolution_add_fusion.5), channel_id=1, source_target_pairs={{0,8},{1,9},{2,10},{3,11},{4,12},{5,13},{6,14},{7,15},{8,0},{9,1},... | collective-permute-start | bytes 2359304 | tf_op jit(solution)/shard_map/ppermute | solution.py:77
  85.6 6.7 %collective-permute-start.26 = (f32[2,32,512]{2,1,0:T(8,128)S(1)}, f32[2,32,512]{2,1,0:T(8,128)S(1)}, u32[]{:S(2)}, u32[]{:S(2)}) collective-permute-start(f32[2,32,512]{2,1,0:T(8,128)S(1)} %bitcast.141), channel_id=1, source_target_pairs={{0,64},{16,80},{32,96},{48,112},{64,0},{80,16},{96,32},{112,48},{1... | collective-permute-start | bytes 393224 | tf_op jit(solution)/shard_map/ppermute | solution.py:91
  92.3 5.7 %collective-permute-start.27 = (f32[2,2,32,512]{3,2,0,1:T(8,128)S(1)}, f32[2,2,32,512]{3,2,0,1:T(8,128)S(1)}, u32[]{:S(2)}, u32[]{:S(2)}) collective-permute-start(f32[2,2,32,512]{3,2,0,1:T(8,128)S(1)} %pad_maximum_fusion.2), channel_id=1, source_target_pairs={{0,32},{16,48},{32,0},{48,16},{64,96},{80,112},{96,64},{112,80},{1... | collective-permute-start | bytes 786440 | tf_op jit(solution)/shard_map/ppermute | solution.py:91
  98.1 11.1 %collective-permute-start.28 = (f32[2,2,2,32,512]{4,3,0,1,2:T(8,128)S(1)}, f32[2,2,2,32,512]{4,3,0,1,2:T(8,128)S(1)}, u32[]{:S(2)}, u32[]{:S(2)}) collective-permute-start(f32[2,2,2,32,512]{4,3,0,1,2:T(8,128)S(1)} %pad_maximum_fusion.1), channel_id=1, source_target_pairs={{0,16},{16,0},{32,48},{48,32},{64,80},{80,64},{96,112},{112,96},{1... | collective-permute-start | bytes 1572872 | tf_op jit(solution)/shard_map/ppermute | solution.py:91
  (9 other events, 112.2 us)
